TPU v7x, 256 devices: a whole 4x4x8 slice. The times are simulated.
256 devices in a mesh: grp: 2 (over z_lo), gy: 16 (over y, x), gx: 8 (over z_hi, core).
Axes of the slice: x: 4, y: 4, z: 8 (z_hi: 4, z_lo: 2; z = z_hi * 2 + z_lo), core: 2. Of those that a mesh axis runs over, the one named last changes fastest.
Arguments:
- state_in: float32 [2, 60, 160, 320], P('grp', None, 'gy', 'gx'), may hold values from -6 to 6
- cotangent: float32 [2, 60, 160, 320], P('grp', None, 'gy', 'gx'), may hold values from -6 to 6
- faces: float32 [2, 2, 160, 320], P('grp', None, 'gy', 'gx'), may hold values from 0.02 to 0.2
- mixing: float32 [2, 60, 60], P('grp'), may hold values from 0 to 0.008
- anchor_row: int32 [1], replicated, may hold values from 0 to 144
- anchor_col: int32 [1], replicated, may hold values from 0 to 288
Outputs:
- tangent_out: float32 [2, 60, 160, 320], P('grp', None, 'gy', 'gx')
- adjoint_out: float32 [2, 60, 160, 320], P('grp', None, 'gy', 'gx')
Inputs may be any that keep to these rules, and one draw needn't show every extreme that they name: `anchor_row`: the zoom region lies wholly inside the parent grid. `anchor_col`: the zoom region lies wholly inside the parent grid.
All inputs are finite; a program needn't handle non-finite values.
Results may differ from a plain program's by a relative error of at most 0.0001.
Values sent between devices are 32-bit elements; how exact they have to be, the bound alone decides.
A program may use at most 64 MiB of HBM per device.

v0:
```python
import jax
import jax.numpy as jnp
from jax import lax
from jax.sharding import PartitionSpec as P

SUB = 10
R = 10
FRAME = 2


def shifted(block, axis, distance):
    devices = range(lax.axis_size(axis))
    route = [(i - distance, i) for i in devices if i - distance in devices]
    return lax.ppermute(block, axis, route)


def extended(cells, sides, width):
    for axis, dim in sides:
        count = lax.axis_size(axis)
        ends = count - 1
        head = lax.slice_in_dim(cells, 0, width, axis=dim)
        tail = lax.slice_in_dim(cells, cells.shape[dim] - width, cells.shape[dim], axis=dim)
        cells = jnp.concatenate(
            [
                lax.ppermute(tail, axis, [(i, (i + 1) % count) for i in range(ends)]),
                cells,
                lax.ppermute(head, axis, [((i + 1) % count, i) for i in range(ends)]),
            ],
            axis=dim,
        )
    return cells


def mix_down(field, matrix):
    return jnp.einsum("lm,myx->lyx", matrix, field, precision=lax.Precision.HIGHEST) + 0.75 * field


def mix_up(field, matrix):
    return jnp.einsum("ml,myx->lyx", matrix, field, precision=lax.Precision.HIGHEST) + 0.75 * field


def shards(state_in, cotangent, faces, mixing, anchor_row, anchor_col):
    levels = state_in.shape[1]
    height = state_in.shape[2]
    width = state_in.shape[3]
    tiles_y = lax.axis_size("gy")
    tiles_x = lax.axis_size("gx")
    total_rows = height * tiles_y
    total_cols = width * tiles_x
    box_rows = total_rows // R
    box_cols = total_cols // R
    block_rows = height // R
    block_cols = width // R
    is_zoom = lax.axis_index("grp") == 1
    tile_y = lax.axis_index("gy")
    tile_x = lax.axis_index("gx")
    rows = tile_y * height + jnp.arange(height, dtype=jnp.int32)
    cols = tile_x * width + jnp.arange(width, dtype=jnp.int32)
    east_face = jnp.where(cols[None, :] == total_cols - 1, jnp.float32(0.0), faces[0, 0])
    north_face = jnp.where(rows[:, None] == total_rows - 1, jnp.float32(0.0), faces[0, 1])
    west_column = shifted(east_face[:, width - 1 :], "gx", 1)
    west_face = jnp.concatenate([west_column, east_face[:, :-1]], axis=1)
    south_line = shifted(north_face[height - 1 :, :], "gy", 1)
    south_face = jnp.concatenate([south_line, north_face[:-1, :]], axis=0)
    matrix = mixing[0]
    edge = (
        (rows[:, None] < FRAME)
        | (rows[:, None] >= total_rows - FRAME)
        | (cols[None, :] < FRAME)
        | (cols[None, :] >= total_cols - FRAME)
    )
    frame = edge.astype(jnp.float32)
    inside = 1.0 - frame
    first_row = anchor_row[0]
    first_col = anchor_col[0]
    box_local_rows = first_row + jnp.arange(box_rows, dtype=jnp.int32) - tile_y * height
    box_local_cols = first_col + jnp.arange(box_cols, dtype=jnp.int32) - tile_x * width
    owned_rows = (box_local_rows >= 0) & (box_local_rows < height)
    owned_cols = (box_local_cols >= 0) & (box_local_cols < width)
    tile_box_rows = rows - first_row
    tile_box_cols = cols - first_col
    within_rows = (tile_box_rows >= 0) & (tile_box_rows < box_rows)
    within_cols = (tile_box_cols >= 0) & (tile_box_cols < box_cols)
    within = within_rows[:, None] & within_cols[None, :]
    zero_index = jnp.zeros((), jnp.int32)
    block_start = (zero_index, tile_y * block_rows, tile_x * block_cols)

    def diffuse(field):
        padded = extended(field, (("gy", 1), ("gx", 2)), 1)
        east = padded[:, 1:-1, 2:]
        west = padded[:, 1:-1, :-2]
        north = padded[:, 2:, 1:-1]
        south = padded[:, :-2, 1:-1]
        return (
            field
            + east_face * (east - field)
            - west_face * (field - west)
            + north_face * (north - field)
            - south_face * (field - south)
        )

    def to_zoom(field):
        picked = jnp.take(field, jnp.clip(box_local_rows, 0, height - 1), axis=1)
        picked = jnp.take(picked, jnp.clip(box_local_cols, 0, width - 1), axis=2)
        owned = owned_rows[:, None] & owned_cols[None, :] & jnp.logical_not(is_zoom)
        term = jnp.where(owned[None], picked, jnp.float32(0.0))
        partial_box = lax.psum(term, ("gy", "gx"))
        whole_box = shifted(partial_box, "grp", 1)
        return lax.dynamic_slice(whole_box, block_start, (levels, block_rows, block_cols))

    def inject_tile(piece):
        return jnp.repeat(jnp.repeat(piece, R, axis=1), R, axis=2)

    def to_global(tile_values):
        crossed = shifted(tile_values, "grp", -1)
        pieces = lax.all_gather(crossed[None], ("gy", "gx"), axis=0, tiled=True)
        pieces = pieces.reshape(tiles_y, tiles_x, levels, block_rows, block_cols)
        return pieces.transpose(2, 0, 3, 1, 4).reshape(levels, box_rows, box_cols)

    def overlay(box, fallback):
        picked = jnp.take(box, jnp.clip(tile_box_rows, 0, box_rows - 1), axis=1)
        picked = jnp.take(picked, jnp.clip(tile_box_cols, 0, box_cols - 1), axis=2)
        return jnp.where(within[None], picked, fallback)

    coarse = mix_down(diffuse(state_in[0]), matrix)
    boundary = inject_tile(to_zoom(coarse))
    fine = coarse * inside + boundary * frame

    def forward(substep, current):
        current = mix_down(diffuse(current), matrix)
        return current * inside + boundary * frame

    fine = lax.fori_loop(0, SUB - 1, forward, fine)
    averages = fine.reshape(levels, block_rows, R, block_cols, R).mean(axis=(2, 4))
    coarse_box = to_global(averages)
    tangent = jnp.where(is_zoom, fine, overlay(coarse_box, coarse))
    forcing = cotangent[0]
    adjoint_fine = forcing + inject_tile(to_zoom(forcing)) / (R * R)
    collected = jnp.zeros((levels, block_rows, block_cols), jnp.float32)

    def backward(substep, carry):
        current, gathered = carry
        gathered = gathered + (current * frame).reshape(levels, block_rows, R, block_cols, R).sum(
            axis=(2, 4)
        )
        current = diffuse(mix_up(current * inside, matrix))
        return (current, gathered)

    adjoint_fine, collected = lax.fori_loop(0, SUB, backward, (adjoint_fine, collected))
    parent_box = to_global(collected)
    adjoint_coarse = diffuse(mix_up(overlay(parent_box, forcing), matrix))
    adjoint = jnp.where(is_zoom, adjoint_fine, adjoint_coarse)
    return (tangent[None], adjoint[None])


def solution(mesh):
    placed = (
        P("grp", None, "gy", "gx"),
        P("grp", None, "gy", "gx"),
        P("grp", None, "gy", "gx"),
        P("grp", None, None),
        P(),
        P(),
    )
    return jax.shard_map(
        shards,
        mesh=mesh,
        in_specs=placed,
        out_specs=(P("grp", None, "gy", "gx"), P("grp", None, "gy", "gx")),
        check_vma=False,
    )
```

profile of v0, /device:TPU:1, one launch (start us, length us, event | category | flops | bytes accessed | tf_op | source)
XLA Modules:
  0.0 2127.4 jit_solution(17732748442739219944)
XLA Ops:
  8.0 3.9 collective-permute-start.8
  14.1 4.0 collective-permute-start.13
  18.2 6.3 collective-permute-start.11
  33.2 5.1 collective-permute-done.10
  44.4 1252.1 %all-reduce.3.cloned.1.call-done = (f32[60,16,32]{0,1,2:T(8,128)}, f32[60,16,32]{0,1,2:T(8,128)}) async-done(((f32[60,16,32]{0,1,2:T(8,128)}, f32[60,16,32]{0,1,2:T(8,128)}), (f32[60,16,32]{0,1,2:T(8,128)}, f32[60,16,32]{0,1,2:T(8,128)})) %all-reduce.3.cloned.1.call-update) | async-done | bytes 245776 | tf_op jit(solution)/shard_map/psum | solution.py:107
  1303.2 5.6 collective-permute-done.16
  1308.9 180.5 %while.28 = (s32[]{:T(128)}, f32[60,10,40]{0,2,1:T(8,128)S(1)}, f32[60,1,4]{0,2,1:T(4,128)S(1)}, f32[60,60]{1,0:T(8,128)S(1)}, f32[10,40]{1,0:T(8,128)S(1)}, /*i...) while((s32[]{:T(128)}, f32[60,10,40]{0,2,1:T(8,128)S(1)}, ...), condition=%wide.region_9.14_spmd.clone.clone.clone, body=%wide.region_6.13_spmd.clone.clone.clone.sunk | while | flops 17909920 | bytes 834095 | solution.py:149
  1315.2 4.1 collective-permute-start.6
  1421.1 4.6 collective-permute-done.7
  1426.5 4.1 collective-permute-start.4
  1441.1 4.6 collective-permute-done.7
  1446.5 5.7 collective-permute-start.4
  1462.8 4.5 collective-permute-done.7
  1468.3 5.7 collective-permute-start.4
  1484.5 4.5 collective-permute-done.7
  1491.0 177.1 %while.27 = (s32[]{:T(128)}, f32[60,10,40]{0,2,1:T(8,128)S(1)}, f32[10,40]{1,0:T(8,128)S(1)}, f32[10,40]{1,0:T(8,128)S(1)}, f32[10,40]{1,0:T(8,128)S(1)}, /*inde...) while((s32[]{:T(128)}, f32[60,10,40]{0,2,1:T(8,128)S(1)}, ...), condition=%wide.region_2.5_spmd.clone.clone, body=%wide.region_1.4_spmd.clone.clone.sunk | while | flops 18170800 | bytes 1191817 | solution.py:133
  1491.0 5.7 collective-permute-start
  1507.2 4.5 collective-permute-done.3
  1526.7 4.5 collective-permute-done.3
  1546.1 4.5 collective-permute-done.3
  1565.6 4.6 collective-permute-done.3
  1585.0 4.6 collective-permute-done.3
  1598.6 3.9 collective-permute-start.2
  1604.5 4.6 collective-permute-done.3
  1623.9 4.6 collective-permute-done.3
  1643.4 4.6 collective-permute-done.3
  1662.9 4.6 collective-permute-done.3
  1669.5 209.5 %all-gather.1 = f32[7680,1,4]{2,1,0:T(1,128)} all-gather(f32[60,1,4]{2,1,0:T(1,128)S(1)} %collective-permute-done.17), channel_id=3, replica_groups=mesh['grp'=2,'gy'=16,'gx'=8] {'gy','gx'}, dimensions={0}, use_global_device_ids=true | all-gather | bytes 123840 | tf_op jit(solution)/shard_map/all_gather | solution.py:116
  1878.9 7.0 copy.59
  1886.6 206.3 %all-gather = f32[7680,1,4]{2,1,0:T(1,128)} all-gather(f32[60,1,4]{2,1,0:T(1,128)S(1)} %copy.51), channel_id=2, replica_groups=mesh['grp'=2,'gy'=16,'gx'=8] {'gy','gx'}, dimensions={0}, use_global_device_ids=true | all-gather | bytes 123840 | tf_op jit(solution)/shard_map/all_gather | solution.py:116
  2092.8 7.0 copy.52
  2108.6 5.1 collective-permute-start.21
  (401 shorter events, 309.5 us)
Async XLA Ops:
  7.2 1289.3 %all-reduce.3.cloned.1.call-start = ((), (), s32[]{:S(2)}) async-start(), calls=%async_computation | async-start | bytes 1048576 | tf_op jit(solution)/shard_map/psum | solution.py:107
  8.0 19.8 collective-permute-start.8
  11.9 15.8 collective-permute-start.9
  14.1 19.1 collective-permute-start.13
  18.2 9.5 collective-permute-start.11
  31.3 7.0 collective-permute-start.10
  1296.5 6.7 collective-permute-start.14
  1299.4 9.4 collective-permute-start.16
  1315.2 7.4 collective-permute-start.6
  1419.1 6.6 collective-permute-start.7
  1439.1 6.6 collective-permute-start.7
  1446.5 7.1 collective-permute-start.4
  1460.8 6.6 collective-permute-start.7
  1468.3 7.1 collective-permute-start.4
  1482.5 6.6 collective-permute-start.7
  1489.5 179.9 %collective-permute-start.17 = (f32[60,1,4]{2,1,0:T(1,128)S(1)}, f32[60,1,4]{2,1,0:T(1,128)S(1)}, u32[]{:S(2)}, u32[]{:S(2)}) collective-permute-start(f32[60,1,4]{2,1,0:T(1,128)S(1)} %copy.58), channel_id=1, source_target_pairs={{128,0},{129,1},{130,2},{131,3},{132,4},{133,5},{134,6},{135,7},{1... | collective-permute-start | bytes 2888 | tf_op jit(solution)/shard_map/ppermute | solution.py:14
  1491.0 7.1 collective-permute-start
  1505.2 6.6 collective-permute-start.3
  1524.7 6.6 collective-permute-start.3
  1544.1 6.6 collective-permute-start.3
  1563.6 6.6 collective-permute-start.3
  1579.1 5.9 collective-permute-start.2
  1583.0 6.6 collective-permute-start.3
  1598.6 5.9 collective-permute-start.2
  1602.5 6.6 collective-permute-start.3
  1618.1 5.9 collective-permute-start.2
  1621.9 6.6 collective-permute-start.3
  1637.5 5.9 collective-permute-start.2
  1641.4 6.6 collective-permute-start.3
  1660.8 6.6 collective-permute-start.3
  1668.1 218.3 %collective-permute-start.15 = (f32[60,1,4]{0,2,1:T(4,128)S(1)}, f32[60,1,4]{0,2,1:T(4,128)S(1)}, u32[]{:S(2)}, u32[]{:S(2)}) collective-permute-start(f32[60,1,4]{0,2,1:T(4,128)S(1)} %multiply_bitcast_fusion), channel_id=1, source_target_pairs={{128,0},{129,1},{130,2},{131,3},{132,4},{133,5},{134,6},{135,7},{1... | collective-permute-start | bytes 2888 | tf_op jit(solution)/shard_map/ppermute | solution.py:14
  2108.6 7.8 collective-permute-start.21
  (61 other events, 2814.9 us)
Sparse Core Ops, SparseCore 0:
  44.4 1252.0 all-reduce.2
where the time goes:
time: 2130 us
  waiting for transfers between devices  1410 us (66%)
  blocking collectives  416 us (20%)
  starting transfers between devices  233 us (11%)
  local copies, waits for them, and re-layouts  23.4 us (1%)
    psum x1, waiting for transfers between devices, to_zoom(): partial_box = lax.psum(term, ('gy', 'gx'))  1250 us
    all_gather x2, blocking collectives, to_global(): pieces = lax.all_gather(crossed[None], ('gy', 'gx'), axis=0, tiled=True)  416 us
    ppermute x42, waiting for transfers between devices, extended(): lax.ppermute(head, axis, [((i + 1) % count, i) for i in range(ends)])  153 us
    ppermute x42, starting transfers between devices, extended(): lax.ppermute(tail, axis, [(i, (i + 1) % count) for i in range(ends)])  147 us
    ppermute x42, starting transfers between devices, extended(): lax.ppermute(head, axis, [((i + 1) % count, i) for i in range(ends)])  68.8 us
  transfers between devices with their start and end apart: 91, of which 44 were waited for; matrix products, arithmetic and copies ran while one was open for 1% of the time, Pallas kernels for 0%

commit v1 on v0

v1 whole, which is shorter than its diff:
```python
import functools

import jax
import jax.numpy as jnp
from jax import lax
from jax.experimental import pallas as pl
from jax.experimental.pallas import tpu as pltpu
from jax.sharding import PartitionSpec as P

MESH = pl.DeviceIdType.MESH
HIGHEST = lax.Precision.HIGHEST
F32 = jnp.float32
VMEM = pltpu.VMEM
L = 60
H = 10
W = 40
NY = 160
NX = 320
GY = 16
GX = 8
FRAME = 2
LV = 64
NB = 24
YS = LV + NB


def dot(a, b):
    return lax.dot_general(a, b, (((1,), (0,)), ((), ())), precision=HIGHEST, preferred_element_type=F32)


def dot_t(a, b):
    return lax.dot_general(a, b, (((1,), (1,)), ((), ())), precision=HIGHEST, preferred_element_type=F32)


def gather_kernel(
    anchor_ref, z_ref, chunk_ref, own_ref, cols_ref,
    ext_ref, patch_ref, north_ref, south_ref, east_ref, west_ref,
    strip_out, strip_in, part, pad, send, got,
    strip_s, strip_r, ns_s, ns_r, a_s, a_r, ring_s, ring_r, b_s, b_r,
):
    grp = lax.axis_index("grp")
    gy = lax.axis_index("gy")
    gx = lax.axis_index("gx")
    up = lax.rem(gy + 1, GY)
    down = lax.rem(gy + GY - 1, GY)
    right = lax.rem(gx + 1, GX)
    left = lax.rem(gx + GX - 1, GX)
    barrier = pltpu.get_barrier_semaphore()

    def hello(*where):
        pl.semaphore_signal(barrier, inc=1, device_id=where, device_id_type=MESH)

    def cross(j, c):
        hello(1 - grp, j, gx)
        return c

    lax.fori_loop(0, GY, cross, 0)
    hello(grp, up, gx)
    hello(grp, down, gx)

    @pl.when(grp == 1)
    def _():
        hello(grp, gy, left)
        hello(grp, gy, right)
        pl.semaphore_wait(barrier, GY + 4)

    @pl.when(grp == 0)
    def _():
        def peer(k, c):
            hello(grp, gy, lax.rem(gx + k, GX))
            return c

        lax.fori_loop(1, GX, peer, 0)
        pl.semaphore_wait(barrier, GY + 2 + GX - 1)

    def b_copy(zy, py):
        return pltpu.make_async_remote_copy(
            src_ref=send.at[zy], dst_ref=got.at[py], send_sem=b_s.at[zy], recv_sem=b_r.at[py],
            device_id=(1, zy, gx), device_id_type=MESH,
        )

    @pl.when(grp == 1)
    def _():
        lane = lax.broadcasted_iota(jnp.int32, (LV, 128), 1) % 64
        for q in range(2):
            east = jnp.zeros((LV, 128), F32)
            west = jnp.zeros((LV, 128), F32)
            for k in range(5):
                row = z_ref[5 * q + k]
                here = (lane >= 10 * k) & (lane < 10 * k + 10)
                east = jnp.where(here, pltpu.roll(row, (10 * k - 40) % 128, 1), east)
                west = jnp.where(here, pltpu.roll(row, (10 * k - 10) % 128, 1), west)
            strip_out[0, q] = east
            strip_out[1, q] = west
        sides = []
        for s, to in ((0, right), (1, left)):
            copy = pltpu.make_async_remote_copy(
                src_ref=strip_out.at[s], dst_ref=strip_in.at[s], send_sem=strip_s.at[s], recv_sem=strip_r.at[s],
                device_id=(1, gy, to), device_id_type=MESH,
            )
            copy.start()
            sides.append(copy)
        for copy in sides:
            copy.wait()
        for q in range(2):
            from_west = strip_in[0, q]
            from_east = strip_in[1, q]
            for k in range(5):
                row = z_ref[5 * q + k]
                row = jnp.where(lane < 10, pltpu.roll(from_west, (-10 * k) % 128, 1), row)
                row = jnp.where((lane >= 50) & (lane < 60), pltpu.roll(from_east, (50 - 10 * k) % 128, 1), row)
                ext_ref[H + 5 * q + k] = row
        ends = []
        for s, to in ((0, up), (1, down)):
            copy = pltpu.make_async_remote_copy(
                src_ref=ext_ref.at[pl.ds(H, H)], dst_ref=ext_ref.at[pl.ds(2 * H * s, H)],
                send_sem=ns_s.at[s], recv_sem=ns_r.at[s],
                device_id=(1, to, gx), device_id_type=MESH,
            )
            copy.start()
            ends.append(copy)

        def arrive(py, total):
            b_copy(gy, py).wait_recv()
            return total + got[py]

        patch_ref[...] = lax.fori_loop(0, GY, arrive, jnp.zeros((5, 8, 128), F32))
        for copy in ends:
            copy.wait()

    @pl.when(grp == 0)
    def _():
        def a_copy(to, sender):
            return pltpu.make_async_remote_copy(
                src_ref=chunk_ref.at[to], dst_ref=part.at[sender], send_sem=a_s.at[to], recv_sem=a_r.at[sender],
                device_id=(0, gy, to), device_id_type=MESH,
            )

        def a_start(k, c):
            a_copy(lax.rem(gx + k, GX), gx).start()
            return c

        lax.fori_loop(1, GX, a_start, 0)
        ring = []
        for s, (src, dst, where) in enumerate((
            (own_ref.at[H - 1], south_ref, (0, up, gx)),
            (own_ref.at[0], north_ref, (0, down, gx)),
            (cols_ref.at[1], west_ref, (0, gy, right)),
            (cols_ref.at[0], east_ref, (0, gy, left)),
        )):
            copy = pltpu.make_async_remote_copy(
                src_ref=src, dst_ref=dst, send_sem=ring_s.at[s], recv_sem=ring_r.at[s],
                device_id=where, device_id_type=MESH,
            )
            copy.start()
            ring.append(copy)

        def a_arrive(k, total):
            sender = lax.rem(gx + k, GX)
            a_copy(gx, sender).wait_recv()
            return total + part[sender]

        total = lax.fori_loop(1, GX, a_arrive, chunk_ref[gx])
        pad[0:5] = jnp.zeros((5, 8, 128), F32)
        pad[15:20] = jnp.zeros((5, 8, 128), F32)
        pad[5:15] = total
        offset = anchor_ref[0] - 2 - H * gy + 5

        def b_start(zy, c):
            start = jnp.clip(zy + offset, 0, 15)
            for i in range(5):
                send[zy, i] = pad[start + i]
            b_copy(zy, gy).start()
            return c

        lax.fori_loop(0, GY, b_start, 0)

        def a_sent(k, c):
            a_copy(lax.rem(gx + k, GX), gx).wait_send()
            return c

        lax.fori_loop(1, GX, a_sent, 0)
        for copy in ring:
            copy.wait()

        def b_sent(zy, c):
            b_copy(zy, gy).wait_send()
            return c

        lax.fori_loop(0, GY, b_sent, 0)


def vmem(n):
    return [pl.BlockSpec(memory_space=VMEM)] * n


def smem():
    return pl.BlockSpec(memory_space=pltpu.SMEM)


def gather(anchor, z, chunks, own, cols):
    dma = pltpu.SemaphoreType.DMA
    return pl.pallas_call(
        gather_kernel,
        name="gather",
        out_shape=(
            jax.ShapeDtypeStruct((3 * H, LV, 128), F32),
            jax.ShapeDtypeStruct((5, 8, 128), F32),
            jax.ShapeDtypeStruct((W, 128), F32),
            jax.ShapeDtypeStruct((W, 128), F32),
            jax.ShapeDtypeStruct((16, 128), F32),
            jax.ShapeDtypeStruct((16, 128), F32),
        ),
        in_specs=[smem()] + vmem(4),
        out_specs=tuple(vmem(6)),
        scratch_shapes=[
            VMEM((2, 2, LV, 128), F32),
            VMEM((2, 2, LV, 128), F32),
            VMEM((GX, H, 8, 128), F32),
            VMEM((20, 8, 128), F32),
            VMEM((GY, 5, 8, 128), F32),
            VMEM((GY, 5, 8, 128), F32),
            dma((2,)), dma((2,)), dma((2,)), dma((2,)),
            dma((GX,)), dma((GX,)), dma((4,)), dma((4,)), dma((GY,)), dma((GY,)),
        ],
        compiler_params=pltpu.CompilerParams(collective_id=0, has_side_effects=True, vmem_limit_bytes=32 * 2**20),
    )(anchor, z, chunks, own, cols)


def zoom_kernel(pos_ref, ext_ref, patch_ref, mix_ref, tan_ref, adj_ref, msg_ref, ya, yb, cf, en, bs, ss):
    zy = pos_ref[1]
    zx = pos_ref[2]

    @pl.when(pos_ref[0] == 1)
    def _():
        zoom_body(zy, zx, ext_ref, patch_ref, mix_ref, tan_ref, adj_ref, msg_ref, ya, yb, cf, en, bs, ss)


def zoom_body(zy, zx, ext_ref, patch_ref, mix_ref, tan_ref, adj_ref, msg_ref, ya, yb, cf, en, bs, ss):
    rows = 3 * H
    row2 = lax.broadcasted_iota(jnp.int32, (rows, 128), 0)
    lane2 = lax.broadcasted_iota(jnp.int32, (rows, 128), 1)
    col2 = lane2 % 64
    tangent = lane2 < 64

    def interior(dr, dc):
        gr = row2 + (dr - H) + zy * H
        gc = col2 + (dc - H) + zx * W
        keep = (gr >= FRAME) & (gr < NY - FRAME) & (gc >= FRAME) & (gc < NX - FRAME)
        return jnp.where(keep, F32(1.0), F32(0.0))

    def incoming(dr, dc):
        return jnp.where(tangent, F32(1.0), interior(dr, dc))

    inside = interior(0, 0)
    outgoing = jnp.where(tangent, inside, F32(1.0))
    for i in range(2):
        en[i] = jnp.zeros((48, 128), F32)
    for r in range(rows):
        en[0, 8 + r : 9 + r] = ext_ref[r, L : L + 1]
        en[1, 8 + r : 9 + r] = ext_ref[r, L + 1 : L + 2]
    east = en[0, 8:38]
    west = pltpu.roll(east, 1, 1)
    north = en[1, 8:38]
    south = en[1, 7:37]
    cf[0, 0:rows] = outgoing * incoming(0, 0) * (1.0 - east - west - north - south)
    cf[1, 0:rows] = outgoing * incoming(0, 1) * east
    cf[2, 0:rows] = outgoing * incoming(0, -1) * west
    cf[3, 0:rows] = outgoing * incoming(1, 0) * north
    cf[4, 0:rows] = outgoing * incoming(-1, 0) * south
    cf[5, 0:rows] = 1.0 - inside

    b3 = lax.broadcasted_iota(jnp.int32, (NB, 128), 0)
    lane3 = lax.broadcasted_iota(jnp.int32, (NB, 128), 1)
    column3 = (lane3 % 64) // 10
    for r in range(rows):
        match = (b3 // 8 == r // H) & (b3 % 8 == column3 + 1) & (lane3 % 64 < 60)
        level = jnp.where(lane3 < 64, cf[5, r : r + 1], F32(0.01))
        ya[r, 0:LV] = ext_ref[r]
        ya[r, LV:YS] = jnp.where(match, level, F32(0.0))

    for k in range(10):
        src, dst = (ya, yb) if k % 2 == 0 else (yb, ya)

        def collect(i, total, src=src, k=k):
            line = src[H + i]
            bs[i, k * NB : (k + 1) * NB] = line[LV:YS]
            return total + cf[5, pl.ds(H + i, 1)] * line

        ss[k, 0:YS] = lax.fori_loop(0, H, collect, jnp.zeros((YS, 128), F32))
        ss[k, YS:128] = jnp.zeros((128 - YS, 128), F32)

        def update(r, c, src=src, dst=dst):
            line = src[r]
            dst[r] = (
                cf[0, pl.ds(r, 1)] * line
                + cf[1, pl.ds(r, 1)] * pltpu.roll(line, 127, 1)
                + cf[2, pl.ds(r, 1)] * pltpu.roll(line, 1, 1)
                + cf[3, pl.ds(r, 1)] * src[r + 1]
                + cf[4, pl.ds(r, 1)] * src[r - 1]
            )
            return c

        lax.fori_loop(k + 1, rows - 1 - k, update, 0)

    m1 = mix_ref[...]
    m2 = dot(m1, m1)
    m4 = dot(m2, m2)
    m8 = dot(m4, m4)
    m10 = dot(m8, m2)

    patch = patch_ref[...]
    e3 = jnp.broadcast_to(patch[:, :, L : L + 1], patch.shape)
    n3 = jnp.broadcast_to(patch[:, :, L + 1 : L + 2], patch.shape)
    here = patch[1:4]
    e_here = e3[1:4]
    coarse = (
        here
        + e_here * (pltpu.roll(here, 7, 1) - here)
        - pltpu.roll(e_here, 1, 1) * (here - pltpu.roll(here, 1, 1))
        + n3[1:4] * (patch[2:5] - here)
        - n3[0:3] * (here - patch[0:3])
    ).reshape(NB, 128)
    v0 = jnp.where(lane3 < L, coarse, F32(0.0))
    forcing = jnp.where(lane3 < L, pltpu.roll(here.reshape(NB, 128), 64, 1), F32(0.0))
    v01 = jnp.concatenate([v0, dot_t(v0, m1)], 0)
    v03 = jnp.concatenate([v01, dot_t(v01, m2)], 0)
    v09 = jnp.concatenate([v03, dot_t(v03, m4), dot_t(v01, m8), jnp.zeros((16, 128), F32)], 0)
    boundary_left = jnp.transpose(v09)
    both = m10.T + pltpu.roll(m10, 64, 1)
    force = pltpu.roll(dot(forcing, m10), 64, 1)
    main_left = jnp.transpose(jnp.concatenate([both[0:LV], force, jnp.zeros((128 - YS, 128), F32)], 0))[:, 0:YS]

    total = jnp.zeros((LV, 128), F32)
    for r in range(H):
        bs[r, 240:256] = jnp.zeros((16, 128), F32)
        out = dot(main_left, ya[H + r])
        fine = out[0:LV] + dot(boundary_left[0:LV], bs[r])
        total = total + fine
        tan_ref[:, r, :] = pltpu.roll(fine, 118, 1)[0:L, 0:W]
        adj_ref[:, r, :] = pltpu.roll(out[LV:128], 54, 1)[0:L, 0:W]

    i8 = lax.broadcasted_iota(jnp.int32, (8, 128), 0)
    lane8 = lax.broadcasted_iota(jnp.int32, (8, 128), 1)
    block8 = i8 - 4 * lax.rem(zy, 2)
    pick_tan = jnp.where((lane8 >= 10) & (lane8 < 50) & (lane8 // 10 - 1 == block8), F32(1.0), F32(0.0))
    pick_adj = jnp.where((lane8 >= 74) & (lane8 < 114) & ((lane8 - 64) // 10 - 1 == block8), F32(1.0), F32(0.0))
    averages = dot_t(pick_tan, jnp.concatenate([total, jnp.zeros((64, 128), F32)], 0)) * F32(0.01)
    sums = jnp.concatenate([dot_t(pick_adj, ss[k]) for k in range(10)], 0)
    lane80 = lax.broadcasted_iota(jnp.int32, (80, 128), 1)
    forcing_pad = jnp.concatenate([forcing, jnp.zeros((128 - NB, 128), F32)], 0)
    u = jnp.where(lane80 < L, sums, F32(0.0)) + dot(pltpu.roll(sums, 64, 1), forcing_pad)
    u = [u[8 * k : 8 * k + 8] for k in range(10)]
    p = jnp.concatenate(u[0::2], 0) + dot(jnp.concatenate(u[1::2], 0), m1)
    q = dot(jnp.concatenate([p[8:16], p[24:32]], 0), m2)
    collected = p[0:8] + q[0:8] + dot(p[16:24] + q[8:16], m4) + dot(p[32:40], m8)
    msg_ref[...] = jnp.where(lane8 < L, averages, F32(0.0)) + pltpu.roll(jnp.where(lane8 < L, collected, F32(0.0)), 64, 1)


def zoom(pos, ext, patch, mix):
    field = jax.ShapeDtypeStruct((L, H, W), F32)
    return pl.pallas_call(
        zoom_kernel,
        name="zoom",
        out_shape=(field, field, jax.ShapeDtypeStruct((8, 128), F32)),
        in_specs=[smem()] + vmem(3),
        out_specs=tuple(vmem(3)),
        scratch_shapes=[
            VMEM((3 * H, YS, 128), F32),
            VMEM((3 * H, YS, 128), F32),
            VMEM((6, 32, 128), F32),
            VMEM((2, 48, 128), F32),
            VMEM((H, 256, 128), F32),
            VMEM((10, 128, 128), F32),
        ],
        compiler_params=pltpu.CompilerParams(vmem_limit_bytes=32 * 2**20),
    )(pos, ext, patch, mix)


def spread_kernel(msg_ref, box_ref, got, c_s, c_r, d_s, d_r):
    grp = lax.axis_index("grp")
    gy = lax.axis_index("gy")
    gx = lax.axis_index("gx")
    barrier = pltpu.get_barrier_semaphore()

    def hello(*where):
        pl.semaphore_signal(barrier, inc=1, device_id=where, device_id_type=MESH)

    def cross(j, c):
        hello(1 - grp, j, gx)
        return c

    lax.fori_loop(0, GY, cross, 0)

    @pl.when(grp == 1)
    def _():
        pl.semaphore_wait(barrier, GY)

    @pl.when(grp == 0)
    def _():
        def peer(k, c):
            hello(grp, gy, lax.rem(gx + k, GX))
            return c

        lax.fori_loop(1, GX, peer, 0)
        pl.semaphore_wait(barrier, GY + GX - 1)

    def c_copy(py, zy):
        return pltpu.make_async_remote_copy(
            src_ref=msg_ref, dst_ref=got.at[zy], send_sem=c_s.at[py], recv_sem=c_r.at[zy],
            device_id=(0, py, gx), device_id_type=MESH,
        )

    @pl.when(grp == 1)
    def _():
        def start(k, c):
            c_copy(k, gy).start()
            return c

        lax.fori_loop(0, GY, start, 0)

        def sent(k, c):
            c_copy(k, gy).wait_send()
            return c

        lax.fori_loop(0, GY, sent, 0)

    @pl.when(grp == 0)
    def _():
        def arrive(k, c):
            c_copy(gy, 2 * k).wait_recv()
            c_copy(gy, 2 * k + 1).wait_recv()
            box_ref[gx, k] = got[2 * k] + got[2 * k + 1]
            return c

        lax.fori_loop(0, GY // 2, arrive, 0)

        def d_copy(to, sender):
            return pltpu.make_async_remote_copy(
                src_ref=box_ref.at[gx], dst_ref=box_ref.at[sender], send_sem=d_s.at[to], recv_sem=d_r.at[sender],
                device_id=(0, gy, to), device_id_type=MESH,
            )

        def start(k, c):
            d_copy(lax.rem(gx + k, GX), gx).start()
            return c

        lax.fori_loop(1, GX, start, 0)

        def finish(k, c):
            other = lax.rem(gx + k, GX)
            d_copy(gx, other).wait_recv()
            d_copy(other, gx).wait_send()
            return c

        lax.fori_loop(1, GX, finish, 0)


def spread(msg):
    dma = pltpu.SemaphoreType.DMA
    return pl.pallas_call(
        spread_kernel,
        name="spread",
        out_shape=jax.ShapeDtypeStruct((GX, GY // 2, 8, 128), F32),
        in_specs=vmem(1),
        out_specs=vmem(1)[0],
        scratch_shapes=[VMEM((GY, 8, 128), F32), dma((GY,)), dma((GY,)), dma((GX,)), dma((GX,))],
        compiler_params=pltpu.CompilerParams(collective_id=1, has_side_effects=True),
    )(msg)


def final_kernel(
    pos_ref, box_ref, own_ref, north_ref, south_ref, east_ref, west_ref, mix_ref, tan_ref, adj_ref,
    tan_out, adj_out, g, boxpad,
):
    @pl.when(pos_ref[0] == 1)
    def _():
        tan_out[...] = tan_ref[...]
        adj_out[...] = adj_ref[...]

    @pl.when(pos_ref[0] == 0)
    def _():
        py = pos_ref[1]
        px = pos_ref[2]
        row0 = py * H - 1 - pos_ref[3]
        col0 = px * W - 8 - pos_ref[4]
        for i in range(16):
            boxpad[i, 0:56] = jnp.zeros((56, 128), F32)
            boxpad[i, 88:144] = jnp.zeros((56, 128), F32)
            for z in range(GX):
                half = 4 * (i % 2)
                boxpad[i, 56 + 4 * z : 60 + 4 * z] = box_ref[z, i // 2, half : half + 4]
        g[...] = jnp.zeros(g.shape, F32)
        for r in range(H):
            g[1 + r, 8:48] = own_ref[r]
            g[1 + r, 7:8] = west_ref[r : r + 1]
            g[1 + r, 48:49] = east_ref[r : r + 1]
        g[0, 8:48] = south_ref[...]
        g[H + 1, 8:48] = north_ref[...]

        sub = lax.broadcasted_iota(jnp.int32, (56, 128), 0)
        lane = lax.broadcasted_iota(jnp.int32, (56, 128), 1)
        in_cols = (sub + col0 >= 0) & (sub + col0 < 32)
        start = jnp.clip(col0 + 56, 0, 88)
        r128 = lax.broadcasted_iota(jnp.int32, (128, 128), 0)
        c128 = lax.broadcasted_iota(jnp.int32, (128, 128), 1)
        unit = jnp.where((r128 == c128) & (r128 < 64), F32(1.0), F32(0.0))
        mix = unit + pltpu.roll(jnp.concatenate([jnp.zeros((64, 128), F32), mix_ref[0:64]], 0), 64, 1)

        def one(i, c):
            br = row0 + i
            within = in_cols & (br >= 0) & (br < 16)
            window = boxpad[jnp.clip(br, 0, 15), pl.ds(start, 56)]
            w = jnp.where(within & (lane >= 64), window, g[i])
            g[i] = dot(w, mix)
            return c

        lax.fori_loop(0, H + 2, one, 0)

        def two(r, c):
            y = g[r + 1]
            upper = g[r + 2]
            lower = g[r]
            e = jnp.broadcast_to(y[:, L : L + 1], y.shape)
            n = jnp.broadcast_to(y[:, L + 1 : L + 2], y.shape)
            s = jnp.broadcast_to(lower[:, L + 1 : L + 2], y.shape)
            out = (
                y
                + e * (pltpu.roll(y, 55, 0) - y)
                - pltpu.roll(e, 1, 0) * (y - pltpu.roll(y, 1, 0))
                + n * (upper - y)
                - s * (y - lower)
            )
            br = row0 + r + 1
            within = in_cols & (br >= 0) & (br < 16)
            window = boxpad[jnp.clip(br, 0, 15), pl.ds(start, 56)]
            out = jnp.where(within & (lane < 64), window, out)
            g[r] = out
            return c

        lax.fori_loop(0, H, two, 0)
        for r in range(H):
            flat = jnp.transpose(jnp.concatenate([g[r, 8:48], jnp.zeros((88, 128), F32)], 0))
            tan_out[:, r, :] = flat[0:L, 0:W]
            adj_out[:, r, :] = flat[64 : 64 + L, 0:W]


def final(pos, box, own, north, south, east, west, mix, tan, adj):
    field = jax.ShapeDtypeStruct((L, H, W), F32)
    return pl.pallas_call(
        final_kernel,
        name="final",
        out_shape=(field, field),
        in_specs=[smem()] + vmem(9),
        out_specs=tuple(vmem(2)),
        scratch_shapes=[VMEM((12, 56, 128), F32), VMEM((16, 144, 128), F32)],
        compiler_params=pltpu.CompilerParams(vmem_limit_bytes=32 * 2**20),
    )(pos, box, own, north, south, east, west, mix, tan, adj)


def shards(state_in, cotangent, faces, mixing, anchor_row, anchor_col):
    grp = lax.axis_index("grp")
    gy = lax.axis_index("gy")
    gx = lax.axis_index("gx")
    pos = jnp.stack([grp, gy, gx, anchor_row[0], anchor_col[0]]).astype(jnp.int32)
    state = state_in[0]
    forcing = cotangent[0]
    rows = gy * H + jnp.arange(H, dtype=jnp.int32)
    cols = gx * W + jnp.arange(W, dtype=jnp.int32)
    east = jnp.where(cols[None, :] == NX - 1, F32(0.0), faces[0, 0])
    north = jnp.where(rows[:, None] == NY - 1, F32(0.0), faces[0, 1])
    both = jnp.stack([east, north])
    zeros2 = jnp.zeros((2, H, W), F32)
    mix = jnp.pad(mixing[0] + 0.75 * jnp.eye(L, dtype=F32), ((0, 128 - L), (0, 128 - L)))

    z_tan = jnp.pad(jnp.concatenate([state, both, zeros2], 0), ((0, 0), (0, 0), (H, 64 - H - W)))
    z_adj = jnp.pad(jnp.concatenate([forcing, both, zeros2], 0), ((0, 0), (0, 0), (H, 64 - H - W)))
    z = jnp.concatenate([z_tan, z_adj], 2).transpose(1, 0, 2)

    mixed = jnp.einsum("lm,myx->lyx", mixing[0], state, precision=HIGHEST) + 0.75 * state
    cells = jnp.concatenate([mixed, both, zeros2, forcing, jnp.zeros((4, H, W), F32)], 0)
    own = cells.transpose(1, 2, 0)
    start = jnp.clip(anchor_col[0] - 2 - W * gx, -36, W) + 36
    zero = jnp.zeros((), jnp.int32)
    window = lax.dynamic_slice(jnp.pad(own, ((0, 0), (36, 36), (0, 0))), (zero, start, zero), (H, 36, 128))
    chunks = jnp.stack([window[:, 4 * k : 4 * k + 8] for k in range(GX)])
    ends = jnp.stack([jnp.pad(own[:, 0], ((0, 6), (0, 0))), jnp.pad(own[:, W - 1], ((0, 6), (0, 0)))])

    ext, patch, ring_n, ring_s, ring_e, ring_w = gather(anchor_row, z, chunks, own, ends)
    tan, adj, msg = zoom(pos, ext, patch, mix)
    box = spread(msg)
    tan, adj = final(pos, box, own, ring_n, ring_s, ring_e, ring_w, mix, tan, adj)
    return tan[None], adj[None]


def solution(mesh):
    placed = (
        P("grp", None, "gy", "gx"),
        P("grp", None, "gy", "gx"),
        P("grp", None, "gy", "gx"),
        P("grp", None, None),
        P(),
        P(),
    )
    return jax.shard_map(
        shards,
        mesh=mesh,
        in_specs=placed,
        out_specs=(P("grp", None, "gy", "gx"), P("grp", None, "gy", "gx")),
        check_vma=False,
    )
```

time: 2130 us -> 84.2 us (0.04)
  waiting for transfers between devices: 1410 us -> 0 us
  blocking collectives: 416 us -> 0 us
  starting transfers between devices: 233 us -> 0 us
  Pallas kernels: 0 us -> 74.7 us
    psum x1 -> x0, waiting for transfers between devices: 1250 us -> none  [to_zoom(): partial_box = lax.psum(term, ('gy', 'gx'))]
    all_gather x2 -> x0, blocking collectives: 416 us -> none  [to_global(): pieces = lax.all_gather(crossed[None], ('gy', 'gx'), axis=0, tiled=True)]
    ppermute x90 -> x0, starting transfers between devices: 233 us -> none  [the longest x42 147 us: extended(): lax.ppermute(tail, axis, [(i, (i + 1) % count) for i in range(ends)])]
    ppermute x90 -> x0, waiting for transfers between devices: 161 us -> none  [the longest x42 153 us: extended(): lax.ppermute(head, axis, [((i + 1) % count, i) for i in range(ends)])]
    pallas_call x0 -> x4, Pallas kernels: none -> 74.7 us  [the longest x1 42.5 us: spread(): pl.pallas_call(spread_kernel, name='spread', out_shape=jax.ShapeDtypeStru...]
  transfers between devices with their start and end apart: 91 -> 0, of which waited for: 44 -> 0; matrix products, arithmetic and copies ran while one was open for 1% -> 0% of each run, Pallas kernels for 0% -> 0%
where the time goes in v1:
time: 84.2 us; the launch traced here: 83.9 us
  Pallas kernels  74.7 us (89%)
  local copies, waits for them, and re-layouts  6.19 us (7%)
  between operations  2.26 us (3%)
    pallas_call x1, Pallas kernels, spread(): pl.pallas_call(spread_kernel, name='spread', out_shape=jax.ShapeDtypeStru...  42.5 us
    pallas_call x1, Pallas kernels, gather(): pl.pallas_call(gather_kernel, name='gather', out_shape=(jax.ShapeDtypeStr...  27.2 us
    unnamed x23, local copies, waits for them, and re-layouts  5.16 us
    pallas_call x1, Pallas kernels, final(): pl.pallas_call(final_kernel, name='final', out_shape=(field, field), in_s...  4.45 us

profile of v1, /device:TPU:1, one launch (start us, length us, event | category | flops | bytes accessed | tf_op | source)
XLA Modules:
  0.0 83.9 jit_solution(13678357176080633708)
XLA Ops:
  1.3 0.0 copy-start.5
  1.3 0.0 copy-start.4
  2.0 0.1 stack.54.pos_ref
  2.1 0.0 copy-done.5
  2.1 0.0 copy-done.4
  2.1 0.1 copy.14
  2.3 0.1 copy.15
  2.4 0.0 copy-start.2
  2.4 0.1 broadcast_select_fusion
  2.5 0.8 copy-done.2
  3.4 0.3 fusion.17
  3.7 0.0 copy-start.3
  3.8 0.9 %copy-done.3 = f32[1,60,10,40]{1,3,2,0:T(8,128)S(1)} copy-done((f32[1,60,10,40]{1,3,2,0:T(8,128)S(1)}, f32[1,60,10,40]{1,3,2,0:T(8,128)}, u32[]{:S(2)}) %copy-start.3) | copy-done | bytes 96024
  4.7 0.4 concatenate.18
  5.0 0.2 pad_maximum_fusion.1
  5.3 0.1 fusion
  5.4 0.2 copy.17.z_ref
  5.9 27.2 %gather.1 = (f32[30,64,128]{2,1,0:T(8,128)S(1)}, f32[5,8,128]{2,1,0:T(8,128)S(1)}, f32[40,128]{1,0:T(8,128)S(1)}, f32[40,128]{1,0:T(8,128)S(1)}, f32[16,128]{1,0:T(8,128)S(1)}, /*index=5*/f32[16,128]{1,0:T(8,128)S(1)}) custom-call(s32[1]{0:T(128)S(6)} %copy.39.anchor_ref, f32[10,64,128]{2,1,0:T(8,128)S(1)} %copy.17.z_ref, ...), custom_call_target="tpu_custom_call" | custom-call | tf_op jit(solution)/shard_map/gather/pallas_call | solution.py:203
  33.1 0.6 zoom.1
  33.6 0.0 copy-start.1
  33.6 0.6 copy-done.1
  34.2 42.5 %spread.1.box_ref = f32[8,8,8,128]{3,2,1,0:T(8,128)} custom-call(f32[8,128]{1,0:T(8,128)} %copy-done.1), custom_call_target="tpu_custom_call" | custom-call | tf_op jit(solution)/shard_map/spread/pallas_call | solution.py:461
  76.7 0.0 copy-start
  76.8 0.9 %copy-done = f32[8,8,8,128]{3,2,1,0:T(8,128)S(1)} copy-done((f32[8,8,8,128]{3,2,1,0:T(8,128)S(1)}, f32[8,8,8,128]{3,2,1,0:T(8,128)}, u32[]{:S(2)}) %copy-start) | copy-done | bytes 262168
  77.7 4.5 %final.1 = (f32[60,10,40]{2,1,0:T(8,128)S(1)}, f32[60,10,40]{2,1,0:T(8,128)S(1)}) custom-call(s32[5]{0:T(128)S(1)} %stack.54.pos_ref, f32[8,8,8,128]{3,2,1,0:T(8,128)S(1)} %copy-done, f32[10,40,128]{2,1,0:T(8,128)S(1)} %bitcast.76, f32[40,128]{1,0:T(8,128)S(1)} %get-tuple-element.16.north_ref, f32[40,128]{1,0:T(8,128)S(1)} %get-tuple-element.17.south_ref, ...), custom_call_target="tpu_custom_call" | custom-call | tf_op jit(solution)/shard_map/final/pallas_call | solution.py:550
  82.2 0.9 %copy.18 = f32[1,60,10,40]{1,3,2,0:T(8,128)} copy(f32[1,60,10,40]{3,2,1,0:T(8,128)S(1)} %bitcast.78) | data formatting | bytes 192000
  83.0 0.9 %copy.19 = f32[1,60,10,40]{1,3,2,0:T(8,128)} copy(f32[1,60,10,40]{3,2,1,0:T(8,128)S(1)} %bitcast.77) | data formatting | bytes 192000
  (22 shorter events, 0.3 us)
Async XLA Ops:
  1.3 0.8 copy-start.5
  1.3 0.8 copy-start.4
  2.4 0.9 %copy-start.2 = (f32[1,60,10,40]{1,3,2,0:T(8,128)S(1)}, f32[1,60,10,40]{1,3,2,0:T(8,128)}, u32[]{:S(2)}) copy-start(f32[1,60,10,40]{1,3,2,0:T(8,128)} %param.6) | copy-start | bytes 288004
  3.7 0.9 %copy-start.3 = (f32[1,60,10,40]{1,3,2,0:T(8,128)S(1)}, f32[1,60,10,40]{1,3,2,0:T(8,128)}, u32[]{:S(2)}) copy-start(f32[1,60,10,40]{1,3,2,0:T(8,128)} %param.7) | copy-start | bytes 288004
  33.6 0.6 copy-start.1
  76.7 1.0 %copy-start = (f32[8,8,8,128]{3,2,1,0:T(8,128)S(1)}, f32[8,8,8,128]{3,2,1,0:T(8,128)}, u32[]{:S(2)}) copy-start(f32[8,8,8,128]{3,2,1,0:T(8,128)} %spread.1.box_ref) | copy-start | bytes 786436

commit v2 on v0

v2 whole, which is shorter than its diff:
```python
import jax
import jax.numpy as jnp
from jax import lax
from jax.experimental import pallas as pl
from jax.experimental.pallas import tpu as pltpu
from jax.sharding import PartitionSpec as P

MESH = pl.DeviceIdType.MESH
HIGHEST = lax.Precision.HIGHEST
F32 = jnp.float32
VMEM = pltpu.VMEM
L = 60
H = 10
W = 40
NY = 160
NX = 320
GY = 16
GX = 8
FRAME = 2
SUB = 10
CHUNKS = 4
ROWS = 3 * H
BLOCK = 6
BOX0 = 56


def dot(a, b):
    return lax.dot_general(a, b, (((1,), (0,)), ((), ())), precision=HIGHEST, preferred_element_type=F32)


def dot_t(a, b):
    return lax.dot_general(a, b, (((1,), (1,)), ((), ())), precision=HIGHEST, preferred_element_type=F32)


def iota(shape, dim):
    return lax.broadcasted_iota(jnp.int32, shape, dim)


def only(keep, value=1.0):
    return jnp.where(keep, F32(value), F32(0.0))


def padded_rows(a, rows):
    return jnp.concatenate([a, jnp.zeros((rows - a.shape[0], a.shape[1]), F32)], 0)


def lanes_to_rows(a, count):
    return jnp.concatenate([a[:, 128 * k : 128 * k + 128] for k in range(count)], 0)


def rows_to_lanes(a, count):
    return jnp.concatenate([a[8 * k : 8 * k + 8] for k in range(count)], 1)


def kernel(
    arow_ref, acol_ref, state_hbm, cot_hbm, faces_hbm, mix_hbm,
    out_ref,
    state, cot, faces, mixing, load_s, raw_t, raw_x, square,
    ya, yb, yc, yd, cf, cfb, en, bs, ss, mp, npow, strip_out, strip_in, got, msg,
    cells, pc, ends, part, pad, send, g, ring_n, ring_s, ring_e, ring_w, faces_b, coarse, box, boxpad,
    strip_s, strip_r, ns_s, ns_r, a_s, a_r, ring_snd, ring_rcv, b_s, b_r, c_s, c_r,
):
    grp = lax.axis_index("grp")
    gy = lax.axis_index("gy")
    gx = lax.axis_index("gx")
    up = lax.rem(gy + 1, GY)
    down = lax.rem(gy + GY - 1, GY)
    right = lax.rem(gx + 1, GX)
    left = lax.rem(gx + GX - 1, GX)
    loads = [
        pltpu.make_async_copy(src, dst, load_s.at[i])
        for i, (src, dst) in enumerate(((state_hbm, state), (cot_hbm, cot), (faces_hbm, faces), (mix_hbm, mixing)))
    ]
    for copy in loads:
        copy.start()
    barrier = pltpu.get_barrier_semaphore()

    def hello(*where):
        pl.semaphore_signal(barrier, inc=1, device_id=where, device_id_type=MESH)

    def cross(j, c):
        hello(1 - grp, lax.rem(gy + j, GY), gx)
        return c

    hello(grp, up, gx)
    hello(grp, down, gx)

    @pl.when(grp == 1)
    def _():
        hello(grp, gy, left)
        hello(grp, gy, right)

    @pl.when(grp == 0)
    def _():
        def peer(k, c):
            hello(grp, gy, lax.rem(gx + k, GX))
            return c

        lax.fori_loop(1, GX, peer, 0)

    lax.fori_loop(0, GY, cross, 0)

    raw_t[...] = jnp.zeros(raw_t.shape, F32)
    raw_x[...] = jnp.zeros(raw_x.shape, F32)
    square[...] = jnp.zeros((128, 128), F32)
    for copy in loads:
        copy.wait()
    last_col = gx * W + iota((1, W), 1) == NX - 1
    for r in range(H):
        raw_t[r, 0:L, 0:W] = state[0, :, r, :]
        raw_x[r, 0:L, 0:W] = cot[0, :, r, :]
        east = jnp.where(last_col, F32(0.0), faces[0, 0, r : r + 1, :])
        north = faces[0, 1, r : r + 1, :]
        if r == H - 1:
            north = jnp.where(gy * H + r + 0 * iota((1, W), 1) == NY - 1, F32(0.0), north)
        for raw in (raw_t, raw_x):
            raw[r, L : L + 1, 0:W] = east
            raw[r, L + 1 : L + 2, 0:W] = north
    square[0:L, 0:L] = mixing[0] + only(iota((L, L), 0) == iota((L, L), 1), 0.75)

    def b_copy(zy, py):
        return pltpu.make_async_remote_copy(
            src_ref=send.at[zy], dst_ref=got.at[py], send_sem=b_s.at[zy], recv_sem=b_r.at[py],
            device_id=(1, zy, gx), device_id_type=MESH,
        )

    @pl.when(grp == 1)
    def _():
        zoom(
            gy, gx, up, down, left, right, barrier, b_copy, out_ref, raw_t, raw_x, square,
            ya, yb, yc, yd, cf, cfb, en, bs, ss, mp, npow, strip_out, strip_in, got, msg, box,
            strip_s, strip_r, ns_s, ns_r, c_s, c_r,
        )

    @pl.when(grp == 0)
    def _():
        parent(
            gy, gx, up, down, left, right, barrier, b_copy, arow_ref, acol_ref, out_ref, raw_t, raw_x, square,
            cells, pc, ends, part, pad, send, g, ring_n, ring_s, ring_e, ring_w, faces_b, coarse, msg, box, boxpad,
            a_s, a_r, ring_snd, ring_rcv, c_s, c_r,
        )


def sweep(src, dst, cfb, k):
    low, high = k + 1, ROWS - 1 - k
    while low < high:
        n = min(BLOCK, high - low)
        line = src[low : low + n]
        dst[low : low + n] = (
            cfb[0, low : low + n] * line
            + cfb[1, low : low + n] * pltpu.roll(line, 127, 3)
            + cfb[2, low : low + n] * pltpu.roll(line, 1, 3)
            + cfb[3, low : low + n] * src[low + 1 : low + n + 1]
            + cfb[4, low : low + n] * src[low - 1 : low + n - 1]
        )
        low += n


def frame_sum(src, cfb):
    return jnp.sum(cfb[5, H : 2 * H] * src[H : 2 * H], axis=0)


def zoom(
    zy, zx, up, down, left, right, barrier, b_copy, out_ref, raw_t, raw_x, square,
    ya, yb, yc, yd, cf, cfb, en, bs, ss, mp, npow, strip_out, strip_in, got, msg, box,
    strip_s, strip_r, ns_s, ns_r, c_s, c_r,
):
    lane = iota((64, 128), 1)
    lane64 = lane % 64
    for r in range(H):
        row = jnp.where((lane >= 10) & (lane < 50), pltpu.roll(raw_t[r], 10, 1), F32(0.0))
        row = jnp.where((lane >= 74) & (lane < 114), pltpu.roll(raw_x[r], 74, 1), row)
        raw_t[r] = row
    for q in range(2):
        east = jnp.zeros((64, 128), F32)
        west = jnp.zeros((64, 128), F32)
        for k in range(5):
            row = raw_t[5 * q + k]
            here = (lane64 >= 10 * k) & (lane64 < 10 * k + 10)
            east = jnp.where(here, pltpu.roll(row, (10 * k - 40) % 128, 1), east)
            west = jnp.where(here, pltpu.roll(row, (10 * k - 10) % 128, 1), west)
        strip_out[0, :, q] = east.reshape(CHUNKS, 2, 8, 128)
        strip_out[1, :, q] = west.reshape(CHUNKS, 2, 8, 128)
    pl.semaphore_wait(barrier, GY + 4)

    def strip_copy(s, c):
        return pltpu.make_async_remote_copy(
            src_ref=strip_out.at[s, c], dst_ref=strip_in.at[s, c], send_sem=strip_s.at[s, c], recv_sem=strip_r.at[s, c],
            device_id=(1, zy, (right, left)[s]), device_id_type=MESH,
        )

    def end_copy(s, c):
        return pltpu.make_async_remote_copy(
            src_ref=ya.at[c, pl.ds(H, H)], dst_ref=ya.at[c, pl.ds(2 * H * s, H)],
            send_sem=ns_s.at[s, c], recv_sem=ns_r.at[s, c],
            device_id=(1, (up, down)[s], zx), device_id_type=MESH,
        )

    order = (3, 0, 1, 2)
    for c in order:
        for s in range(2):
            strip_copy(s, c).start()
    lane16 = iota((2, 8, 128), 2)
    for c in order:
        for s in range(2):
            strip_copy(s, c).wait_recv()
        for q in range(2):
            from_west = strip_in[0, c, q]
            from_east = strip_in[1, c, q]
            for k in range(5):
                row = raw_t[5 * q + k, 16 * c : 16 * c + 16].reshape(2, 8, 128)
                row = jnp.where(lane16 % 64 < 10, pltpu.roll(from_west, (-10 * k) % 128, 2), row)
                here = (lane16 % 64 >= 50) & (lane16 % 64 < 60)
                row = jnp.where(here, pltpu.roll(from_east, (50 - 10 * k) % 128, 2), row)
                ya[c, H + 5 * q + k] = row
        for s in range(2):
            end_copy(s, c).start()

    m1 = square[...]
    unit = only(iota((128, 128), 0) == iota((128, 128), 1))
    p01 = jnp.concatenate([unit, m1], 0)
    mp[0:256] = p01
    m2 = dot(m1, m1)
    mp[256:512] = dot(p01, m2)
    m4 = dot(m2, m2)
    mp[512:1024] = dot(mp[0:512], m4)
    m8 = dot(m4, m4)
    mp[1024:1280] = dot(p01, m8)
    mp[1280:1408] = dot(m8, m2)

    def flip(k, c):
        npow[k] = jnp.transpose(mp[pl.ds(pl.multiple_of(128 * k, 128), 128)])
        return c

    lax.fori_loop(0, SUB + 1, flip, 0)

    row2 = iota((ROWS, 128), 0)
    lane2 = iota((ROWS, 128), 1)
    tangent = lane2 < 64

    def interior(dr, dc):
        gr = row2 + (dr - H) + zy * H
        gc = lane2 % 64 + (dc - H) + zx * W
        return only((gr >= FRAME) & (gr < NY - FRAME) & (gc >= FRAME) & (gc < NX - FRAME))

    def incoming(dr, dc):
        return jnp.where(tangent, F32(1.0), interior(dr, dc))

    inside = interior(0, 0)
    outgoing = jnp.where(tangent, inside, F32(1.0))
    edge = 1.0 - inside
    for r in range(ROWS):
        cfb[5, r, 0] = jnp.broadcast_to(edge[r : r + 1], (8, 128))
    star = jnp.where(zy == 1, 0, jnp.where(zy == GY - 2, 2, 1))
    other0 = jnp.where(zy == 1, 1, 0)
    other1 = jnp.where(zy == GY - 2, 1, 2)
    corner = jnp.where(zx == 0, 2, 5)
    sub8 = iota((8, 128), 0)
    lane8 = iota((8, 128), 1)
    column8 = (lane8 % 64) // 10 + 1
    for r in range(ROWS):
        br = r // H
        middle = (sub8 >= 1) & (sub8 <= 6) & (column8 == sub8) & (star + 0 * sub8 == br)
        first = (sub8 == 0) & (column8 == corner) & (other0 + 0 * sub8 == br)
        second = (sub8 == 7) & (column8 == corner) & (other1 + 0 * sub8 == br)
        tan_slot = jnp.where((middle | first | second) & (lane8 < 60), cfb[5, r, 0], F32(0.0))
        adj_slot = only((column8 == sub8) & (lane8 >= 64) & (lane8 < 124), 0.01)
        for b in range(3):
            value = adj_slot if b == br else jnp.zeros((8, 128), F32)
            yc[r, b] = value + tan_slot if b == 0 else value

    for s in range(2):
        end_copy(s, 3).wait()
    for i in range(2):
        en[i] = jnp.zeros((48, 128), F32)
        for r in range(ROWS):
            en[i, 8 + r : 9 + r] = ya[3, r, 1, 4 + i : 5 + i]
    east = en[0, 8:38]
    west = pltpu.roll(east, 1, 1)
    north = en[1, 8:38]
    south = en[1, 7:37]
    cf[0, 0:ROWS] = outgoing * incoming(0, 0) * (1.0 - east - west - north - south)
    cf[1, 0:ROWS] = outgoing * incoming(0, 1) * east
    cf[2, 0:ROWS] = outgoing * incoming(0, -1) * west
    cf[3, 0:ROWS] = outgoing * incoming(1, 0) * north
    cf[4, 0:ROWS] = outgoing * incoming(-1, 0) * south
    for i in range(5):
        for r in range(ROWS):
            cfb[i, r, 0] = jnp.broadcast_to(cf[i, r : r + 1], (8, 128))

    for k in range(SUB):
        src, dst = (yc, yd) if k % 2 == 0 else (yd, yc)
        bs[:, k] = src[H : 2 * H, 0]
        ss[k, 8:11] = frame_sum(src, cfb)
        ss[k, 11:16] = jnp.zeros((5, 8, 128), F32)
        sweep(src, dst, cfb, k)

    def chunk(i, carry):
        c = lax.rem(i + 3, CHUNKS)

        @pl.when(i > 0)
        def _():
            for s in range(2):
                end_copy(s, c).wait()

        for k in range(SUB):
            src, dst = (ya.at[c], yb) if k % 2 == 0 else (yb, ya.at[c])
            ss[k, pl.ds(2 * c, 2)] = frame_sum(src, cfb)
            sweep(src, dst, cfb, k)
        return carry

    lax.fori_loop(0, CHUNKS, chunk, 0)

    pick_tan = only((lane8 >= 10) & (lane8 < 50) & (lane8 // 10 - 1 == sub8), 0.01)
    pick_adj = only((lane8 >= 74) & (lane8 < 114) & ((lane8 - 64) // 10 - 1 == sub8))
    sums = dot_t(pick_adj, ss[...].reshape(SUB * 128, 128))
    lanes = iota((8, SUB * 128), 1) % 128
    own_sum = dot(jnp.where(lanes < L, sums, F32(0.0)), mp[0 : SUB * 128])
    share = pltpu.roll(lanes_to_rows(sums, SUB), 64, 1)
    level_sum = jnp.sum(ya[:, H : 2 * H], axis=1).reshape(64, 128)
    slot_sum = jnp.sum(bs[...], axis=0).reshape(8 * SUB, 128)
    mean_of = dot_t(pick_tan, jnp.concatenate([level_sum, slot_sum[0:64]], 0))
    tail_of = dot_t(pick_tan, padded_rows(slot_sum[64:80], 128))
    own_mean = dot(jnp.where(lane8 < L, mean_of, F32(0.0)), npow[SUB])
    slot_mean = jnp.where(lane8 < 64, pltpu.roll(mean_of, 64, 1), pltpu.roll(tail_of, 64, 1))

    def arrive(py, total):
        b_copy(zy, py).wait_recv()
        return total + got[py]

    patch = lax.fori_loop(0, GY, arrive, jnp.zeros((5, 8, 128), F32))
    e3 = jnp.broadcast_to(patch[:, :, L : L + 1], patch.shape)
    n3 = jnp.broadcast_to(patch[:, :, L + 1 : L + 2], patch.shape)
    here = patch[1:4]
    e_here = e3[1:4]
    values = (
        here
        + e_here * (pltpu.roll(here, 7, 1) - here)
        - pltpu.roll(e_here, 1, 1) * (here - pltpu.roll(here, 1, 1))
        + n3[1:4] * (patch[2:5] - here)
        - n3[0:3] * (here - patch[0:3])
    )
    values = jnp.where(iota((3, 8, 128), 2) < L, values, F32(0.0))
    flag = zy + 0 * sub8
    main = jnp.where(flag == 1, values[0], jnp.where(flag == GY - 2, values[2], values[1]))
    side0 = jnp.where(flag == 1, values[1], values[0])
    side1 = jnp.where(flag == GY - 2, values[1], values[2])
    west_most = zx + 0 * iota((1, 128), 1) == 0
    side0 = jnp.where(west_most, side0[2:3], side0[5:6])
    side1 = jnp.where(west_most, side1[2:3], side1[5:6])
    v0 = jnp.where(sub8 == 0, side0, jnp.where(sub8 == 7, side1, main))
    forcing = jnp.where(iota((24, 128), 1) < L, pltpu.roll(here.reshape(24, 128), 64, 1), F32(0.0))
    powers = jnp.concatenate([dot(v0, npow[k]) for k in range(SUB)], 0)
    given = dot(share, padded_rows(forcing, 128))
    collected = own_sum + dot(rows_to_lanes(given, SUB), mp[0 : SUB * 128])
    averages = own_mean + dot(slot_mean, padded_rows(powers, 128))
    line = jnp.where(lane8 < 64, averages, pltpu.roll(collected, 64, 1))
    msg[...] = line[0:4]
    me = zy * GX + zx

    def c_start(i, c):
        pltpu.make_async_remote_copy(
            src_ref=msg, dst_ref=box.at[me], send_sem=c_s.at[0], recv_sem=c_r.at[0],
            device_id=(0, lax.rem(zy + i // GX, GY), lax.rem(zx + i, GX)), device_id_type=MESH,
        ).start()
        return c

    lax.fori_loop(0, GY * GX, c_start, 0)

    m10 = mp[1280:1408]
    both = npow[SUB] + pltpu.roll(m10, 64, 1)
    force = pltpu.roll(dot(forcing, m10), 64, 1)
    head = jnp.concatenate([both[0:64], force, powers[0:40]], 0)
    left_side = jnp.concatenate([jnp.transpose(head), jnp.transpose(padded_rows(powers[40:80], 128))], 1)[:, 0:168]
    for r in range(H):
        right_side = jnp.concatenate(
            [ya[:, H + r].reshape(64, 128), yc[H + r].reshape(24, 128), bs[r].reshape(80, 128)], 0
        )
        res = dot(left_side, right_side)
        out_ref[r, 0:64] = pltpu.roll(res[0:64], 118, 1)
        out_ref[r, 64:128] = pltpu.roll(res[64:128], 54, 1)
    for c in order:
        for s in range(2):
            strip_copy(s, c).wait_send()
    pltpu.make_async_remote_copy(
        src_ref=box, dst_ref=box, send_sem=c_s.at[0], recv_sem=c_r.at[0], device_id=(0, zy, zx), device_id_type=MESH
    ).wait_send()


def parent(
    py, px, up, down, left, right, barrier, b_copy, arow_ref, acol_ref, out_ref, raw_t, raw_x, square,
    cells, pc, ends, part, pad, send, g, ring_n, ring_s, ring_e, ring_w, faces_b, coarse, msg, box, boxpad,
    a_s, a_r, ring_snd, ring_rcv, c_s, c_r,
):
    r128 = iota((128, 128), 0)
    c128 = iota((128, 128), 1)
    for r in range(H):
        cells[r * W : (r + 1) * W] = jnp.transpose(jnp.concatenate([raw_t[r], raw_x[r]], 0))[0:W]
        pc[r, 0:40] = jnp.zeros((40, 128), F32)
        pc[r, 80:120] = jnp.zeros((40, 128), F32)
    mixed = dot(cells[...], jnp.transpose(square[...]) + only((r128 == c128) & (r128 >= L)))
    for r in range(H):
        pc[r, 40:80] = mixed[r * W : (r + 1) * W]
    ends[...] = jnp.zeros((2, 16, 128), F32)
    for r in range(H):
        ends[0, r : r + 1] = pc[r, 40:41]
        ends[1, r : r + 1] = pc[r, 79:80]
    start = jnp.clip(acol_ref[0] - 2 - W * px, -36, W) + 40
    for z in range(GX):
        part[z] = pc[:, pl.ds(start + 4 * z, 8)]
    g[...] = jnp.zeros(g.shape, F32)
    pl.semaphore_wait(barrier, GY + 2 + GX - 1)

    def a_copy(to, sender):
        return pltpu.make_async_remote_copy(
            src_ref=part.at[to], dst_ref=part.at[GX + sender], send_sem=a_s.at[to], recv_sem=a_r.at[sender],
            device_id=(0, py, to), device_id_type=MESH,
        )

    def a_start(k, c):
        a_copy(lax.rem(px + k, GX), px).start()
        return c

    lax.fori_loop(1, GX, a_start, 0)
    ring = []
    for s, (src, dst, where) in enumerate((
        (pc.at[H - 1, pl.ds(40, W)], ring_s, (0, up, px)),
        (pc.at[0, pl.ds(40, W)], ring_n, (0, down, px)),
        (ends.at[1], ring_w, (0, py, right)),
        (ends.at[0], ring_e, (0, py, left)),
    )):
        copy = pltpu.make_async_remote_copy(
            src_ref=src, dst_ref=dst, send_sem=ring_snd.at[s], recv_sem=ring_rcv.at[s],
            device_id=where, device_id_type=MESH,
        )
        copy.start()
        ring.append(copy)
    pad[0:5] = jnp.zeros((5, 8, 128), F32)
    pad[15:20] = jnp.zeros((5, 8, 128), F32)

    def a_arrive(k, total):
        sender = lax.rem(px + k, GX)
        a_copy(px, sender).wait_recv()
        return total + part[GX + sender]

    pad[5:15] = lax.fori_loop(1, GX, a_arrive, part[px])
    offset = arow_ref[0] - 2 - H * py + 5

    def b_start(j, c):
        zy = lax.rem(py + j, GY)
        first = jnp.clip(zy + offset, 0, 15)
        for i in range(5):
            send[zy, i] = pad[first + i]
        b_copy(zy, py).start()
        return c

    lax.fori_loop(0, GY, b_start, 0)

    for copy in ring:
        copy.wait()
    g[0, 8:48] = ring_s[...]
    g[H + 1, 8:48] = ring_n[...]
    for r in range(H):
        g[1 + r, 8:48] = pc[r, 40:80]
        g[1 + r, 7:8] = ring_w[r : r + 1]
        g[1 + r, 48:49] = ring_e[r : r + 1]
    for r in range(H):
        y = g[r + 1]
        e = jnp.broadcast_to(y[:, L : L + 1], y.shape)
        n = jnp.broadcast_to(y[:, L + 1 : L + 2], y.shape)
        s = jnp.broadcast_to(g[r][:, L + 1 : L + 2], y.shape)
        w = pltpu.roll(e, 1, 0)
        faces_b[0, r] = e
        faces_b[1, r] = w
        faces_b[2, r] = n
        faces_b[3, r] = s
        coarse[r] = (
            y + e * (pltpu.roll(y, 55, 0) - y) - w * (y - pltpu.roll(y, 1, 0)) + n * (g[r + 2] - y) - s * (y - g[r])
        )
    for i in range(16):
        boxpad[i, 0:BOX0] = jnp.zeros((BOX0, 128), F32)
        boxpad[i, BOX0 + 32 : 144] = jnp.zeros((56, 128), F32)
    down_mix = pltpu.roll(jnp.concatenate([jnp.zeros((64, 128), F32), square[0:64]], 0), 64, 1)
    row0 = py * H - 1 - arow_ref[0]
    col0 = px * W - 8 - acol_ref[0]
    sub = iota((56, 128), 0)
    lane = iota((56, 128), 1)
    in_cols = (sub + col0 >= 0) & (sub + col0 < 32)
    first = jnp.clip(col0 + BOX0, 0, 88)

    def a_sent(k, c):
        a_copy(lax.rem(px + k, GX), px).wait_send()
        return c

    lax.fori_loop(1, GX, a_sent, 0)

    def b_sent(zy, c):
        b_copy(zy, py).wait_send()
        return c

    lax.fori_loop(0, GY, b_sent, 0)

    pltpu.make_async_remote_copy(
        src_ref=box, dst_ref=box, send_sem=c_s.at[0], recv_sem=c_r.at[0], device_id=(1, py, px), device_id_type=MESH
    ).wait_recv()
    for i in range(16):
        for z in range(GX):
            boxpad[i, BOX0 + 4 * z : BOX0 + 4 + 4 * z] = box[GX * i + z]
    windows = []
    for i in range(H + 2):
        br = row0 + i
        within = in_cols & (br + 0 * sub >= 0) & (br + 0 * sub < 16)
        window = boxpad[jnp.clip(br, 0, 15), pl.ds(first, 56)]
        w = jnp.where(within, window, g[i])
        g[i] = w
        if 1 <= i <= H:
            coarse[i - 1] = jnp.where(within, window, coarse[i - 1])
    y_all = dot(g[...].reshape((H + 2) * 56, 128), down_mix).reshape(H + 2, 56, 128)
    for r in range(H):
        y = y_all[r + 1]
        res = (
            y
            + faces_b[0, r] * (pltpu.roll(y, 55, 0) - y)
            - faces_b[1, r] * (y - pltpu.roll(y, 1, 0))
            + faces_b[2, r] * (y_all[r + 2] - y)
            - faces_b[3, r] * (y - y_all[r])
        )
        res = jnp.where(lane < 64, coarse[r], res)
        out_ref[r] = jnp.transpose(padded_rows(res[8:48], 128))


def shards(state_in, cotangent, faces, mixing, anchor_row, anchor_col):
    dma = pltpu.SemaphoreType.DMA
    smem = pl.BlockSpec(memory_space=pltpu.SMEM)
    hbm = pl.BlockSpec(memory_space=pl.ANY)
    out = pl.pallas_call(
        kernel,
        name="step",
        out_shape=jax.ShapeDtypeStruct((H, 128, 128), F32),
        in_specs=[smem, smem, hbm, hbm, hbm, hbm],
        out_specs=pl.BlockSpec(memory_space=VMEM),
        scratch_shapes=[
            VMEM((1, L, H, W), F32),
            VMEM((1, L, H, W), F32),
            VMEM((1, 2, H, W), F32),
            VMEM((1, L, L), F32),
            dma((4,)),
            VMEM((H, 64, 128), F32),
            VMEM((H, 64, 128), F32),
            VMEM((128, 128), F32),
            VMEM((CHUNKS, ROWS, 2, 8, 128), F32),
            VMEM((ROWS, 2, 8, 128), F32),
            VMEM((ROWS, 3, 8, 128), F32),
            VMEM((ROWS, 3, 8, 128), F32),
            VMEM((5, 32, 128), F32),
            VMEM((6, ROWS, 1, 8, 128), F32),
            VMEM((2, 48, 128), F32),
            VMEM((H, SUB, 8, 128), F32),
            VMEM((SUB, 16, 8, 128), F32),
            VMEM((11 * 128, 128), F32),
            VMEM((11, 128, 128), F32),
            VMEM((2, CHUNKS, 2, 2, 8, 128), F32),
            VMEM((2, CHUNKS, 2, 2, 8, 128), F32),
            VMEM((GY, 5, 8, 128), F32),
            VMEM((4, 128), F32),
            VMEM((H * W, 128), F32),
            VMEM((H, 120, 128), F32),
            VMEM((2, 16, 128), F32),
            VMEM((2 * GX, H, 8, 128), F32),
            VMEM((20, 8, 128), F32),
            VMEM((GY, 5, 8, 128), F32),
            VMEM((H + 2, 56, 128), F32),
            VMEM((W, 128), F32),
            VMEM((W, 128), F32),
            VMEM((16, 128), F32),
            VMEM((16, 128), F32),
            VMEM((4, H, 56, 128), F32),
            VMEM((H, 56, 128), F32),
            VMEM((GY * GX, 4, 128), F32),
            VMEM((16, 144, 128), F32),
            dma((2, CHUNKS)), dma((2, CHUNKS)), dma((2, CHUNKS)), dma((2, CHUNKS)),
            dma((GX,)), dma((GX,)), dma((4,)), dma((4,)), dma((GY,)), dma((GY,)), dma((1,)), dma((1,)),
        ],
        compiler_params=pltpu.CompilerParams(collective_id=0, has_side_effects=True, vmem_limit_bytes=40 * 2**20),
    )(anchor_row, anchor_col, state_in, cotangent, faces, mixing)
    tangent = out[:, 0:L, 0:W].transpose(1, 0, 2)
    adjoint = out[:, 64 : 64 + L, 0:W].transpose(1, 0, 2)
    return tangent[None], adjoint[None]


def solution(mesh):
    placed = (
        P("grp", None, "gy", "gx"),
        P("grp", None, "gy", "gx"),
        P("grp", None, "gy", "gx"),
        P("grp", None, None),
        P(),
        P(),
    )
    return jax.shard_map(
        shards,
        mesh=mesh,
        in_specs=placed,
        out_specs=(P("grp", None, "gy", "gx"), P("grp", None, "gy", "gx")),
        check_vma=False,
    )
```

time: 2130 us -> 48.3 us (0.02)
  waiting for transfers between devices: 1410 us -> 0 us
  blocking collectives: 416 us -> 0 us
  starting transfers between devices: 233 us -> 0 us
  Pallas kernels: 0 us -> 41.3 us
    psum x1 -> x0, waiting for transfers between devices: 1250 us -> none  [to_zoom(): partial_box = lax.psum(term, ('gy', 'gx'))]
    all_gather x2 -> x0, blocking collectives: 416 us -> none  [to_global(): pieces = lax.all_gather(crossed[None], ('gy', 'gx'), axis=0, tiled=True)]
    ppermute x90 -> x0, starting transfers between devices: 233 us -> none  [the longest x42 147 us: extended(): lax.ppermute(tail, axis, [(i, (i + 1) % count) for i in range(ends)])]
    ppermute x90 -> x0, waiting for transfers between devices: 161 us -> none  [the longest x42 153 us: extended(): lax.ppermute(head, axis, [((i + 1) % count, i) for i in range(ends)])]
    pallas_call x0 -> x1, Pallas kernels: none -> 41.3 us  [shards(): pl.pallas_call(kernel, name='step', out_shape=jax.ShapeDtypeStruct((H, 12...]
  transfers between devices with their start and end apart: 91 -> 0, of which waited for: 44 -> 0; matrix products, arithmetic and copies ran while one was open for 1% -> 0% of each run, Pallas kernels for 0% -> 0%
where the time goes in v2:
time: 48.3 us; the launch traced here: 48 us
  Pallas kernels  41.3 us (86%)
  local copies, waits for them, and re-layouts  4.76 us (10%)
  between operations  1.95 us (4%)
    pallas_call x1, Pallas kernels, shards(): pl.pallas_call(kernel, name='step', out_shape=jax.ShapeDtypeStruct((H, 12...  41.3 us
    unnamed x8, local copies, waits for them, and re-layouts  4.7 us

profile of v2, /device:TPU:1, one launch (start us, length us, event | category | flops | bytes accessed | tf_op | source)
XLA Modules:
  0.0 48.0 jit_solution(18069210284350984584)
XLA Ops:
  1.9 0.7 %copy.10.faces_hbm = f32[1,2,10,40]{3,2,1,0:T(8,128)S(1)} copy(f32[1,2,10,40]{3,1,2,0:T(2,128)} %param.8) | data formatting | bytes 6400 | tf_op args[2]
  2.6 0.8 %copy.11.mix_hbm = f32[1,60,60]{2,1,0:T(8,128)S(1)} copy(f32[1,60,60]{2,0,1:T(1,128)} %param.9) | data formatting | bytes 28800 | tf_op args[3]
  3.4 0.0 copy-start
  3.4 1.3 %copy.8.state_hbm = f32[1,60,10,40]{3,2,1,0:T(8,128)S(1)} copy(f32[1,60,10,40]{1,3,2,0:T(8,128)} %param.6) | data formatting | bytes 192000 | tf_op args[0]
  4.6 0.0 copy-done
  4.7 0.3 copy.9.cot_hbm
  4.9 41.3 %step.1 = f32[10,128,128]{2,1,0:T(8,128)S(1)} custom-call(s32[1]{0:T(128)S(6)} %copy.14.arow_ref, s32[1]{0:T(128)S(6)} %copy.15.acol_ref, f32[1,60,10,40]{3,2,1,0:T(8,128)S(1)} %copy.8.state_hbm, f32[1,60,10,40]{3,2,1,0:T(8,128)S(1)} %copy.9.cot_hbm, f32[1,2,10,40]{3,2,1,0:T(8,128)S(1)} %copy.10.faces_hbm, f32[1,60,60]{2,1,0:T(8,128)S(1)} %copy.11.mix_hbm), custom_call_target="tpu_custom_call" | custom-call | tf_op jit(solution)/shard_map/step/pallas_call | solution.py:536
  46.3 0.1 slice_bitcast_fusion
  46.3 0.8 %copy.13 = f32[1,60,10,40]{1,3,2,0:T(8,128)} copy(f32[1,60,10,40]{3,1,2,0:T(8,128)S(1)} %get-tuple-element.4) | data formatting | bytes 192000
  47.2 0.8 %copy.12 = f32[1,60,10,40]{1,3,2,0:T(8,128)} copy(f32[1,60,10,40]{3,1,2,0:T(8,128)S(1)} %get-tuple-element.5) | data formatting | bytes 192000
Async XLA Ops:
  3.4 1.3 %copy-start = (f32[1,60,10,40]{1,3,2,0:T(8,128)S(1)}, f32[1,60,10,40]{1,3,2,0:T(8,128)}, u32[]{:S(2)}) copy-start(f32[1,60,10,40]{1,3,2,0:T(8,128)} %param.7) | copy-start | bytes 288004

commit v3 on v2

--- a/solution.py
+++ b/solution.py
@@ -55,8 +55,8 @@
 def kernel(
     arow_ref, acol_ref, state_hbm, cot_hbm, faces_hbm, mix_hbm,
     out_ref,
-    state, cot, faces, mixing, load_s, raw_t, raw_x, square,
-    ya, yb, yc, yd, cf, cfb, en, bs, ss, mp, npow, strip_out, strip_in, got, msg,
+    state, cot, faces, mixing, load_s, raw, mixed_rows, wide, square,
+    ya, yb, yc, yd, cf, cfb, en, bs, ss, power, strip_out, strip_in, got, msg,
     cells, pc, ends, part, pad, send, g, ring_n, ring_s, ring_e, ring_w, faces_b, coarse, box, boxpad,
     strip_s, strip_r, ns_s, ns_r, a_s, a_r, ring_snd, ring_rcv, b_s, b_r, c_s, c_r,
 ):
@@ -100,23 +100,23 @@
 
     lax.fori_loop(0, GY, cross, 0)
 
-    raw_t[...] = jnp.zeros(raw_t.shape, F32)
-    raw_x[...] = jnp.zeros(raw_x.shape, F32)
     square[...] = jnp.zeros((128, 128), F32)
+    wide[...] = jnp.zeros(wide.shape, F32)
+
+    @pl.when(grp == 1)
+    def _():
+        mixed_rows[...] = jnp.zeros(mixed_rows.shape, F32)
+
     for copy in loads:
         copy.wait()
-    last_col = gx * W + iota((1, W), 1) == NX - 1
-    for r in range(H):
-        raw_t[r, 0:L, 0:W] = state[0, :, r, :]
-        raw_x[r, 0:L, 0:W] = cot[0, :, r, :]
-        east = jnp.where(last_col, F32(0.0), faces[0, 0, r : r + 1, :])
-        north = faces[0, 1, r : r + 1, :]
-        if r == H - 1:
-            north = jnp.where(gy * H + r + 0 * iota((1, W), 1) == NY - 1, F32(0.0), north)
-        for raw in (raw_t, raw_x):
-            raw[r, L : L + 1, 0:W] = east
-            raw[r, L + 1 : L + 2, 0:W] = north
-    square[0:L, 0:L] = mixing[0] + only(iota((L, L), 0) == iota((L, L), 1), 0.75)
+    diagonal = iota((1, L), 1)
+    for i in range(L):
+        square[i : i + 1, 0:L] = mixing[i] + only(diagonal == i, 0.75)
+    col = gx * W + iota((H, 2, W), 2)
+    row = gy * H + iota((H, 2, W), 0)
+    kind = iota((H, 2, W), 1)
+    closed = ((kind == 0) & (col == NX - 1)) | ((kind == 1) & (row == NY - 1))
+    wide[:, :, 0:W] = jnp.where(closed, F32(0.0), faces[...])
 
     def b_copy(zy, py):
         return pltpu.make_async_remote_copy(
@@ -127,15 +127,15 @@
     @pl.when(grp == 1)
     def _():
         zoom(
-            gy, gx, up, down, left, right, barrier, b_copy, out_ref, raw_t, raw_x, square,
-            ya, yb, yc, yd, cf, cfb, en, bs, ss, mp, npow, strip_out, strip_in, got, msg, box,
+            gy, gx, up, down, left, right, barrier, b_copy, out_ref, state, cot, wide, mixed_rows, raw, square,
+            ya, yb, yc, yd, cf, cfb, en, bs, ss, power, strip_out, strip_in, got, msg, box,
             strip_s, strip_r, ns_s, ns_r, c_s, c_r,
         )
 
     @pl.when(grp == 0)
     def _():
         parent(
-            gy, gx, up, down, left, right, barrier, b_copy, arow_ref, acol_ref, out_ref, raw_t, raw_x, square,
+            gy, gx, up, down, left, right, barrier, b_copy, arow_ref, acol_ref, out_ref, state, cot, wide, square,
             cells, pc, ends, part, pad, send, g, ring_n, ring_s, ring_e, ring_w, faces_b, coarse, msg, box, boxpad,
             a_s, a_r, ring_snd, ring_rcv, c_s, c_r,
         )
@@ -161,21 +161,26 @@
 
 
 def zoom(
-    zy, zx, up, down, left, right, barrier, b_copy, out_ref, raw_t, raw_x, square,
-    ya, yb, yc, yd, cf, cfb, en, bs, ss, mp, npow, strip_out, strip_in, got, msg, box,
+    zy, zx, up, down, left, right, barrier, b_copy, out_ref, state, cot, wide, mixed_rows, raw, square,
+    ya, yb, yc, yd, cf, cfb, en, bs, ss, power, strip_out, strip_in, got, msg, box,
     strip_s, strip_r, ns_s, ns_r, c_s, c_r,
 ):
     lane = iota((64, 128), 1)
     lane64 = lane % 64
-    for r in range(H):
-        row = jnp.where((lane >= 10) & (lane < 50), pltpu.roll(raw_t[r], 10, 1), F32(0.0))
-        row = jnp.where((lane >= 74) & (lane < 114), pltpu.roll(raw_x[r], 74, 1), row)
-        raw_t[r] = row
+    for q in range(H // 2):
+        for i in range(2):
+            mixed_rows[q, 10:50, 64 * i : 64 * i + L] = state[2 * q + i]
+            mixed_rows[q, 74:114, 64 * i : 64 * i + L] = cot[2 * q + i]
+        turned = jnp.transpose(mixed_rows[q])
+        for i in range(2):
+            face = wide[2 * q + i]
+            raw[2 * q + i] = turned[64 * i : 64 * i + 64]
+            raw[2 * q + i, L : L + 2] = pltpu.roll(face, 10, 1) + pltpu.roll(face, 74, 1)
     for q in range(2):
         east = jnp.zeros((64, 128), F32)
         west = jnp.zeros((64, 128), F32)
         for k in range(5):
-            row = raw_t[5 * q + k]
+            row = raw[5 * q + k]
             here = (lane64 >= 10 * k) & (lane64 < 10 * k + 10)
             east = jnp.where(here, pltpu.roll(row, (10 * k - 40) % 128, 1), east)
             west = jnp.where(here, pltpu.roll(row, (10 * k - 10) % 128, 1), west)
@@ -208,7 +213,7 @@
             from_west = strip_in[0, c, q]
             from_east = strip_in[1, c, q]
             for k in range(5):
-                row = raw_t[5 * q + k, 16 * c : 16 * c + 16].reshape(2, 8, 128)
+                row = raw[5 * q + k, 16 * c : 16 * c + 16].reshape(2, 8, 128)
                 row = jnp.where(lane16 % 64 < 10, pltpu.roll(from_west, (-10 * k) % 128, 2), row)
                 here = (lane16 % 64 >= 50) & (lane16 % 64 < 60)
                 row = jnp.where(here, pltpu.roll(from_east, (50 - 10 * k) % 128, 2), row)
@@ -216,23 +221,12 @@
         for s in range(2):
             end_copy(s, c).start()
 
-    m1 = square[...]
-    unit = only(iota((128, 128), 0) == iota((128, 128), 1))
-    p01 = jnp.concatenate([unit, m1], 0)
-    mp[0:256] = p01
-    m2 = dot(m1, m1)
-    mp[256:512] = dot(p01, m2)
-    m4 = dot(m2, m2)
-    mp[512:1024] = dot(mp[0:512], m4)
-    m8 = dot(m4, m4)
-    mp[1024:1280] = dot(p01, m8)
-    mp[1280:1408] = dot(m8, m2)
-
-    def flip(k, c):
-        npow[k] = jnp.transpose(mp[pl.ds(pl.multiple_of(128 * k, 128), 128)])
-        return c
-
-    lax.fori_loop(0, SUB + 1, flip, 0)
+    b1 = jnp.transpose(square[...]) + pltpu.roll(jnp.concatenate([jnp.zeros((64, 128), F32), square[0:64]], 0), 64, 1)
+    b2 = dot(b1, b1)
+    b4 = dot(b2, b2)
+    b8 = dot(b4, b4)
+    for i, value in enumerate((b1, b2, b4, b8, dot(b8, b2))):
+        power[i] = value
 
     row2 = iota((ROWS, 128), 0)
     lane2 = iota((ROWS, 128), 1)
@@ -314,15 +308,16 @@
     pick_tan = only((lane8 >= 10) & (lane8 < 50) & (lane8 // 10 - 1 == sub8), 0.01)
     pick_adj = only((lane8 >= 74) & (lane8 < 114) & ((lane8 - 64) // 10 - 1 == sub8))
     sums = dot_t(pick_adj, ss[...].reshape(SUB * 128, 128))
-    lanes = iota((8, SUB * 128), 1) % 128
-    own_sum = dot(jnp.where(lanes < L, sums, F32(0.0)), mp[0 : SUB * 128])
-    share = pltpu.roll(lanes_to_rows(sums, SUB), 64, 1)
+    sums = lanes_to_rows(sums, SUB)
+    lane80 = iota((8 * SUB, 128), 1)
     level_sum = jnp.sum(ya[:, H : 2 * H], axis=1).reshape(64, 128)
     slot_sum = jnp.sum(bs[...], axis=0).reshape(8 * SUB, 128)
-    mean_of = dot_t(pick_tan, jnp.concatenate([level_sum, slot_sum[0:64]], 0))
-    tail_of = dot_t(pick_tan, padded_rows(slot_sum[64:80], 128))
-    own_mean = dot(jnp.where(lane8 < L, mean_of, F32(0.0)), npow[SUB])
-    slot_mean = jnp.where(lane8 < 64, pltpu.roll(mean_of, 64, 1), pltpu.roll(tail_of, 64, 1))
+    means = dot_t(pick_tan, jnp.concatenate([slot_sum, jnp.zeros((48, 128), F32)], 0))
+    means = jnp.concatenate([pltpu.roll(means, (-8 * k) % 128, 1) for k in range(SUB)], 0)
+    weights = jnp.where(lane80 < 32, jnp.where(lane80 < 8, means, pltpu.roll(sums, 72, 1)), F32(0.0))
+    own_sums = pltpu.roll(jnp.where(lane80 < L, sums, F32(0.0)), 64, 1)
+    own_mean = dot_t(pick_tan, padded_rows(level_sum, 128))
+    own_mean = jnp.where(lane8 < L, own_mean, F32(0.0))
 
     def arrive(py, total):
         b_copy(zy, py).wait_recv()
@@ -349,12 +344,14 @@
     side0 = jnp.where(west_most, side0[2:3], side0[5:6])
     side1 = jnp.where(west_most, side1[2:3], side1[5:6])
     v0 = jnp.where(sub8 == 0, side0, jnp.where(sub8 == 7, side1, main))
-    forcing = jnp.where(iota((24, 128), 1) < L, pltpu.roll(here.reshape(24, 128), 64, 1), F32(0.0))
-    powers = jnp.concatenate([dot(v0, npow[k]) for k in range(SUB)], 0)
-    given = dot(share, padded_rows(forcing, 128))
-    collected = own_sum + dot(rows_to_lanes(given, SUB), mp[0 : SUB * 128])
-    averages = own_mean + dot(slot_mean, padded_rows(powers, 128))
-    line = jnp.where(lane8 < 64, averages, pltpu.roll(collected, 64, 1))
+    forcing = jnp.where(iota((24, 128), 1) >= 64, here.reshape(24, 128), F32(0.0))
+    u = dot(weights, padded_rows(jnp.concatenate([v0, forcing], 0), 128)) + own_sums
+    u = [u[8 * k : 8 * k + 8] for k in range(SUB)] + [own_mean]
+    p = dot(jnp.concatenate(u[1::2], 0), power[0])
+    p = [u[2 * i] + p[8 * i : 8 * i + 8] for i in range(5)] + [own_mean]
+    q = dot(jnp.concatenate(p[1::2], 0), power[1])
+    q = [p[2 * i] + q[8 * i : 8 * i + 8] for i in range(3)]
+    line = q[0] + dot(q[1], power[2]) + dot(q[2], power[3])
     msg[...] = line[0:4]
     me = zy * GX + zx
 
@@ -365,20 +362,23 @@
         ).start()
         return c
 
-    lax.fori_loop(0, GY * GX, c_start, 0)
-
-    m10 = mp[1280:1408]
-    both = npow[SUB] + pltpu.roll(m10, 64, 1)
-    force = pltpu.roll(dot(forcing, m10), 64, 1)
-    head = jnp.concatenate([both[0:64], force, powers[0:40]], 0)
+    lax.fori_loop(0, GY * GX, c_start, 0, unroll=8)
+
+    powers = jnp.concatenate([v0, dot(v0, power[0])], 0)
+    last = dot(powers, power[3])
+    powers = jnp.concatenate([powers, dot(powers, power[1])], 0)
+    powers = jnp.concatenate([powers, dot(powers, power[2]), last], 0)
+    both = power[4, 0:64] + power[4, 64:128]
+    force = dot(forcing, power[4])
+    head = jnp.concatenate([both, force, powers[0:40]], 0)
     left_side = jnp.concatenate([jnp.transpose(head), jnp.transpose(padded_rows(powers[40:80], 128))], 1)[:, 0:168]
     for r in range(H):
         right_side = jnp.concatenate(
             [ya[:, H + r].reshape(64, 128), yc[H + r].reshape(24, 128), bs[r].reshape(80, 128)], 0
         )
         res = dot(left_side, right_side)
-        out_ref[r, 0:64] = pltpu.roll(res[0:64], 118, 1)
-        out_ref[r, 64:128] = pltpu.roll(res[64:128], 54, 1)
+        res = jnp.transpose(res)
+        out_ref[r] = jnp.where(iota((W, 128), 1) < 64, res[10:50], res[74:114])
     for c in order:
         for s in range(2):
             strip_copy(s, c).wait_send()
@@ -388,14 +388,18 @@
 
 
 def parent(
-    py, px, up, down, left, right, barrier, b_copy, arow_ref, acol_ref, out_ref, raw_t, raw_x, square,
+    py, px, up, down, left, right, barrier, b_copy, arow_ref, acol_ref, out_ref, state, cot, wide, square,
     cells, pc, ends, part, pad, send, g, ring_n, ring_s, ring_e, ring_w, faces_b, coarse, msg, box, boxpad,
     a_s, a_r, ring_snd, ring_rcv, c_s, c_r,
 ):
     r128 = iota((128, 128), 0)
     c128 = iota((128, 128), 1)
+    turned = jnp.transpose(jnp.concatenate([wide[...].reshape(2 * H, 128), jnp.zeros((128 - 2 * H, 128), F32)], 0))[0:W]
+    lane40 = iota((W, 128), 1)
     for r in range(H):
-        cells[r * W : (r + 1) * W] = jnp.transpose(jnp.concatenate([raw_t[r], raw_x[r]], 0))[0:W]
+        cells[r * W : (r + 1) * W] = jnp.where((lane40 >= L) & (lane40 < L + 2), pltpu.roll(turned, L - 2 * r, 1), F32(0.0))
+        cells[r * W : (r + 1) * W, 0:L] = state[r]
+        cells[r * W : (r + 1) * W, 64 : 64 + L] = cot[r]
         pc[r, 0:40] = jnp.zeros((40, 128), F32)
         pc[r, 80:120] = jnp.zeros((40, 128), F32)
     mixed = dot(cells[...], jnp.transpose(square[...]) + only((r128 == c128) & (r128 >= L)))
@@ -526,27 +530,28 @@
             - faces_b[3, r] * (y - y_all[r])
         )
         res = jnp.where(lane < 64, coarse[r], res)
-        out_ref[r] = jnp.transpose(padded_rows(res[8:48], 128))
+        out_ref[r] = res[8:48]
 
 
 def shards(state_in, cotangent, faces, mixing, anchor_row, anchor_col):
     dma = pltpu.SemaphoreType.DMA
     smem = pl.BlockSpec(memory_space=pltpu.SMEM)
-    hbm = pl.BlockSpec(memory_space=pl.ANY)
+    hbm = pl.BlockSpec(memory_space=pltpu.HBM)
     out = pl.pallas_call(
         kernel,
         name="step",
-        out_shape=jax.ShapeDtypeStruct((H, 128, 128), F32),
+        out_shape=jax.ShapeDtypeStruct((H, W, 128), F32),
         in_specs=[smem, smem, hbm, hbm, hbm, hbm],
         out_specs=pl.BlockSpec(memory_space=VMEM),
         scratch_shapes=[
-            VMEM((1, L, H, W), F32),
-            VMEM((1, L, H, W), F32),
-            VMEM((1, 2, H, W), F32),
-            VMEM((1, L, L), F32),
+            VMEM((H, W, L), F32),
+            VMEM((H, W, L), F32),
+            VMEM((H, 2, W), F32),
+            VMEM((L, 1, L), F32),
             dma((4,)),
             VMEM((H, 64, 128), F32),
-            VMEM((H, 64, 128), F32),
+            VMEM((H // 2, 128, 128), F32),
+            VMEM((H, 2, 128), F32),
             VMEM((128, 128), F32),
             VMEM((CHUNKS, ROWS, 2, 8, 128), F32),
             VMEM((ROWS, 2, 8, 128), F32),
@@ -557,8 +562,7 @@
             VMEM((2, 48, 128), F32),
             VMEM((H, SUB, 8, 128), F32),
             VMEM((SUB, 16, 8, 128), F32),
-            VMEM((11 * 128, 128), F32),
-            VMEM((11, 128, 128), F32),
+            VMEM((5, 128, 128), F32),
             VMEM((2, CHUNKS, 2, 2, 8, 128), F32),
             VMEM((2, CHUNKS, 2, 2, 8, 128), F32),
             VMEM((GY, 5, 8, 128), F32),
@@ -581,11 +585,13 @@
             dma((2, CHUNKS)), dma((2, CHUNKS)), dma((2, CHUNKS)), dma((2, CHUNKS)),
             dma((GX,)), dma((GX,)), dma((4,)), dma((4,)), dma((GY,)), dma((GY,)), dma((1,)), dma((1,)),
         ],
-        compiler_params=pltpu.CompilerParams(collective_id=0, has_side_effects=True, vmem_limit_bytes=40 * 2**20),
-    )(anchor_row, anchor_col, state_in, cotangent, faces, mixing)
-    tangent = out[:, 0:L, 0:W].transpose(1, 0, 2)
-    adjoint = out[:, 64 : 64 + L, 0:W].transpose(1, 0, 2)
-    return tangent[None], adjoint[None]
+        compiler_params=pltpu.CompilerParams(collective_id=0, has_side_effects=True, vmem_limit_bytes=56291328),
+    )(
+        anchor_row, anchor_col, state_in[0].transpose(1, 2, 0), cotangent[0].transpose(1, 2, 0),
+        faces[0].transpose(1, 0, 2), mixing.transpose(1, 0, 2),
+    )
+    both = (out[:, :, 0:L], out[:, :, 64 : 64 + L])
+    return tuple(half.transpose(2, 0, 1)[None] for half in both)
 
 
 def solution(mesh):

time: 48.3 us -> 44.1 us (0.913)
  local copies, waits for them, and re-layouts: 4.76 us -> 1.56 us
  Pallas kernels: 41.3 us -> 40.4 us
    unnamed x8 -> x4, local copies, waits for them, and re-layouts: 4.7 us -> 0.75 us
    pallas_call x1, Pallas kernels: 41.3 us -> 40.4 us  [shards(): pl.pallas_call(kernel, name='step', out_shape=jax.ShapeDtypeStruct((H, W,...]
    broadcast_in_dim x1, local copies, waits for them, and re-layouts: 0.05 us -> 0.81 us  [shards(): return tuple((half.transpose(2, 0, 1)[None] for half in both))]
where the time goes in v3:
time: 44.1 us; the launch traced here: 43.9 us
  Pallas kernels  40.4 us (92%)
  between operations  1.97 us (4%)
  local copies, waits for them, and re-layouts  1.56 us (4%)
    pallas_call x1, Pallas kernels, shards(): pl.pallas_call(kernel, name='step', out_shape=jax.ShapeDtypeStruct((H, W,...  40.4 us

profile of v3, /device:TPU:1, one launch (start us, length us, event | category | flops | bytes accessed | tf_op | source)
XLA Modules:
  0.0 43.9 jit_solution(13572703288805089910)
XLA Ops:
  0.6 0.0 copy-start.1
  1.9 0.0 copy-done.1
  2.0 0.0 copy-start
  2.0 0.7 %copy-done = f32[1,60,60]{2,0,1:T(1,128)S(1)} copy-done((f32[1,60,60]{2,0,1:T(1,128)S(1)}, f32[1,60,60]{2,0,1:T(1,128)}, u32[]{:S(2)}) %copy-start) | copy-done | bytes 14424
  2.7 40.4 %step.1 = f32[10,40,128]{2,1,0:T(8,128)S(1)} custom-call(s32[1]{0:T(128)S(6)} %copy.8.arow_ref, s32[1]{0:T(128)S(6)} %copy.9.acol_ref, f32[10,40,60]{2,1,0:T(8,128)} %bitcast.20, f32[10,40,60]{2,1,0:T(8,128)} %bitcast.21, f32[10,2,40]{2,1,0:T(2,128)S(1)} %bitcast.19, f32[60,1,60]{2,1,0:T(1,128)S(1)} %bitcast.18), custom_call_target="tpu_custom_call" | custom-call | tf_op jit(solution)/shard_map/step/pallas_call | solution.py:540
  43.1 0.8 %slice_bitcast_fusion = (f32[1,60,10,40]{1,3,2,0:T(8,128)}, f32[1,60,10,40]{1,3,2,0:T(8,128)}) fusion(f32[10,40,128]{2,1,0:T(8,128)S(1)} %step.1), kind=kLoop, calls=%fused_computation | loop fusion | bytes 384000 | tf_op jit(solution)/shard_map/broadcast_in_dim | solution.py:594
Async XLA Ops:
  0.6 1.3 %copy-start.1 = (f32[1,2,10,40]{3,1,2,0:T(2,128)S(1)}, f32[1,2,10,40]{3,1,2,0:T(2,128)}, u32[]{:S(2)}) copy-start(f32[1,2,10,40]{3,1,2,0:T(2,128)} %param.8) | copy-start | bytes 9604
  2.0 0.8 %copy-start = (f32[1,60,60]{2,0,1:T(1,128)S(1)}, f32[1,60,60]{2,0,1:T(1,128)}, u32[]{:S(2)}) copy-start(f32[1,60,60]{2,0,1:T(1,128)} %param.9) | copy-start | bytes 43204

commit v4 on v3

--- a/solution.py
+++ b/solution.py
@@ -57,7 +57,7 @@
     out_ref,
     state, cot, faces, mixing, load_s, raw, mixed_rows, wide, square,
     ya, yb, yc, yd, cf, cfb, en, bs, ss, power, strip_out, strip_in, got, msg,
-    cells, pc, ends, part, pad, send, g, ring_n, ring_s, ring_e, ring_w, faces_b, coarse, box, boxpad,
+    cells, rows, ends, row_out, row_in, row_pad, window_out, g, ring_n, ring_s, ring_e, ring_w, faces_b, coarse, box, boxpad,
     strip_s, strip_r, ns_s, ns_r, a_s, a_r, ring_snd, ring_rcv, b_s, b_r, c_s, c_r,
 ):
     grp = lax.axis_index("grp")
@@ -78,27 +78,27 @@
     def hello(*where):
         pl.semaphore_signal(barrier, inc=1, device_id=where, device_id_type=MESH)
 
-    def cross(j, c):
-        hello(1 - grp, lax.rem(gy + j, GY), gx)
-        return c
-
-    hello(grp, up, gx)
-    hello(grp, down, gx)
+    hello(grp, gy, left)
+    hello(grp, gy, right)
 
     @pl.when(grp == 1)
     def _():
-        hello(grp, gy, left)
-        hello(grp, gy, right)
+        hello(grp, up, gx)
+        hello(grp, down, gx)
+
+        def cross(j, c):
+            hello(0, lax.rem(gy + GY - 2 + j // GX, GY), lax.rem(gx + j, GX))
+            return c
+
+        lax.fori_loop(0, 5 * GX, cross, 0)
 
     @pl.when(grp == 0)
     def _():
         def peer(k, c):
-            hello(grp, gy, lax.rem(gx + k, GX))
+            hello(0, lax.rem(gy + k, GY), gx)
             return c
 
-        lax.fori_loop(1, GX, peer, 0)
-
-    lax.fori_loop(0, GY, cross, 0)
+        lax.fori_loop(1, GY, peer, 0)
 
     square[...] = jnp.zeros((128, 128), F32)
     wide[...] = jnp.zeros(wide.shape, F32)
@@ -118,26 +118,20 @@
     closed = ((kind == 0) & (col == NX - 1)) | ((kind == 1) & (row == NY - 1))
     wide[:, :, 0:W] = jnp.where(closed, F32(0.0), faces[...])
 
-    def b_copy(zy, py):
-        return pltpu.make_async_remote_copy(
-            src_ref=send.at[zy], dst_ref=got.at[py], send_sem=b_s.at[zy], recv_sem=b_r.at[py],
-            device_id=(1, zy, gx), device_id_type=MESH,
-        )
-
     @pl.when(grp == 1)
     def _():
         zoom(
-            gy, gx, up, down, left, right, barrier, b_copy, out_ref, state, cot, wide, mixed_rows, raw, square,
+            gy, gx, up, down, left, right, barrier, out_ref, state, cot, wide, mixed_rows, raw, square,
             ya, yb, yc, yd, cf, cfb, en, bs, ss, power, strip_out, strip_in, got, msg, box,
-            strip_s, strip_r, ns_s, ns_r, c_s, c_r,
+            strip_s, strip_r, ns_s, ns_r, b_s, b_r, c_s, c_r,
         )
 
     @pl.when(grp == 0)
     def _():
         parent(
-            gy, gx, up, down, left, right, barrier, b_copy, arow_ref, acol_ref, out_ref, state, cot, wide, square,
-            cells, pc, ends, part, pad, send, g, ring_n, ring_s, ring_e, ring_w, faces_b, coarse, msg, box, boxpad,
-            a_s, a_r, ring_snd, ring_rcv, c_s, c_r,
+            gy, gx, up, down, left, right, barrier, arow_ref, acol_ref, out_ref, state, cot, wide, square,
+            cells, rows, ends, row_out, row_in, row_pad, window_out, got, g, ring_n, ring_s, ring_e, ring_w, faces_b, coarse, msg, box, boxpad,
+            a_s, a_r, ring_snd, ring_rcv, b_s, b_r, c_s, c_r,
         )
 
 
@@ -160,10 +154,14 @@
     return jnp.sum(cfb[5, H : 2 * H] * src[H : 2 * H], axis=0)
 
 
+def far(zy, zx):
+    return (zx == 0) | (zx == GX - 1) | (zy <= 1) | (zy >= GY - 2)
+
+
 def zoom(
-    zy, zx, up, down, left, right, barrier, b_copy, out_ref, state, cot, wide, mixed_rows, raw, square,
+    zy, zx, up, down, left, right, barrier, out_ref, state, cot, wide, mixed_rows, raw, square,
     ya, yb, yc, yd, cf, cfb, en, bs, ss, power, strip_out, strip_in, got, msg, box,
-    strip_s, strip_r, ns_s, ns_r, c_s, c_r,
+    strip_s, strip_r, ns_s, ns_r, b_s, b_r, c_s, c_r,
 ):
     lane = iota((64, 128), 1)
     lane64 = lane % 64
@@ -186,7 +184,7 @@
             west = jnp.where(here, pltpu.roll(row, (10 * k - 10) % 128, 1), west)
         strip_out[0, :, q] = east.reshape(CHUNKS, 2, 8, 128)
         strip_out[1, :, q] = west.reshape(CHUNKS, 2, 8, 128)
-    pl.semaphore_wait(barrier, GY + 4)
+    pl.semaphore_wait(barrier, 4)
 
     def strip_copy(s, c):
         return pltpu.make_async_remote_copy(
@@ -319,11 +317,26 @@
     own_mean = dot_t(pick_tan, padded_rows(level_sum, 128))
     own_mean = jnp.where(lane8 < L, own_mean, F32(0.0))
 
-    def arrive(py, total):
-        b_copy(zy, py).wait_recv()
-        return total + got[py]
-
-    patch = lax.fori_loop(0, GY, arrive, jnp.zeros((5, 8, 128), F32))
+    def row_wait(i):
+        pltpu.make_async_remote_copy(
+            src_ref=got.at[i], dst_ref=got.at[i], send_sem=b_s.at[0], recv_sem=b_r.at[i],
+            device_id=(0, zy, zx), device_id_type=MESH,
+        ).wait_recv()
+
+    for i, absent in ((0, 0), (4, GY - 1)):
+        wanted = far(zy, zx) & (zy != absent)
+
+        @pl.when(wanted)
+        def _():
+            row_wait(i)
+
+        @pl.when(jnp.logical_not(wanted))
+        def _():
+            got[i] = jnp.zeros((GX, 8, 128), F32)
+
+    for i in range(1, 4):
+        row_wait(i)
+    patch = jnp.sum(got[...], axis=1)
     e3 = jnp.broadcast_to(patch[:, :, L : L + 1], patch.shape)
     n3 = jnp.broadcast_to(patch[:, :, L + 1 : L + 2], patch.shape)
     here = patch[1:4]
@@ -388,9 +401,9 @@
 
 
 def parent(
-    py, px, up, down, left, right, barrier, b_copy, arow_ref, acol_ref, out_ref, state, cot, wide, square,
-    cells, pc, ends, part, pad, send, g, ring_n, ring_s, ring_e, ring_w, faces_b, coarse, msg, box, boxpad,
-    a_s, a_r, ring_snd, ring_rcv, c_s, c_r,
+    py, px, up, down, left, right, barrier, arow_ref, acol_ref, out_ref, state, cot, wide, square,
+    cells, rows, ends, row_out, row_in, row_pad, window_out, got, g, ring_n, ring_s, ring_e, ring_w, faces_b, coarse, msg, box, boxpad,
+    a_s, a_r, ring_snd, ring_rcv, b_s, b_r, c_s, c_r,
 ):
     r128 = iota((128, 128), 0)
     c128 = iota((128, 128), 1)
@@ -400,36 +413,47 @@
         cells[r * W : (r + 1) * W] = jnp.where((lane40 >= L) & (lane40 < L + 2), pltpu.roll(turned, L - 2 * r, 1), F32(0.0))
         cells[r * W : (r + 1) * W, 0:L] = state[r]
         cells[r * W : (r + 1) * W, 64 : 64 + L] = cot[r]
-        pc[r, 0:40] = jnp.zeros((40, 128), F32)
-        pc[r, 80:120] = jnp.zeros((40, 128), F32)
     mixed = dot(cells[...], jnp.transpose(square[...]) + only((r128 == c128) & (r128 >= L)))
+    rows[0] = jnp.zeros((W, 128), F32)
+    rows[H + 1] = jnp.zeros((W, 128), F32)
     for r in range(H):
-        pc[r, 40:80] = mixed[r * W : (r + 1) * W]
+        rows[1 + r] = mixed[r * W : (r + 1) * W]
     ends[...] = jnp.zeros((2, 16, 128), F32)
     for r in range(H):
-        ends[0, r : r + 1] = pc[r, 40:41]
-        ends[1, r : r + 1] = pc[r, 79:80]
-    start = jnp.clip(acol_ref[0] - 2 - W * px, -36, W) + 40
-    for z in range(GX):
-        part[z] = pc[:, pl.ds(start + 4 * z, 8)]
+        ends[0, r : r + 1] = rows[1 + r, 0:1]
+        ends[1, r : r + 1] = rows[1 + r, W - 1 : W]
+    for t in range(GY + 2):
+        row_out[t] = rows[jnp.clip(t - 1 + arow_ref[0] - H * py, -1, H) + 1]
+    row_in[0, py] = row_out[py + 1]
     g[...] = jnp.zeros(g.shape, F32)
-    pl.semaphore_wait(barrier, GY + 2 + GX - 1)
-
-    def a_copy(to, sender):
+    row_pad[...] = jnp.zeros(row_pad.shape, F32)
+    pl.semaphore_wait(barrier, 5 * GX + GY - 1 + 2)
+
+    def a_copy(t, extra, to):
         return pltpu.make_async_remote_copy(
-            src_ref=part.at[to], dst_ref=part.at[GX + sender], send_sem=a_s.at[to], recv_sem=a_r.at[sender],
-            device_id=(0, py, to), device_id_type=MESH,
+            src_ref=row_out.at[t], dst_ref=row_in.at[extra, py], send_sem=a_s.at[extra], recv_sem=a_r.at[extra],
+            device_id=(0, to, px), device_id_type=MESH,
         )
 
     def a_start(k, c):
-        a_copy(lax.rem(px + k, GX), px).start()
+        to = lax.rem(py + k, GY)
+        a_copy(to + 1, 0, to).start()
         return c
 
-    lax.fori_loop(1, GX, a_start, 0)
+    for t, to in ((0, 0), (GY + 1, GY - 1)):
+        @pl.when(py != to)
+        def _():
+            a_copy(t, 1, to).start()
+
+        @pl.when(py == to)
+        def _():
+            row_in[1, to] = row_out[t]
+
+    lax.fori_loop(1, GY, a_start, 0)
     ring = []
     for s, (src, dst, where) in enumerate((
-        (pc.at[H - 1, pl.ds(40, W)], ring_s, (0, up, px)),
-        (pc.at[0, pl.ds(40, W)], ring_n, (0, down, px)),
+        (rows.at[H], ring_s, (0, up, px)),
+        (rows.at[1], ring_n, (0, down, px)),
         (ends.at[1], ring_w, (0, py, right)),
         (ends.at[0], ring_e, (0, py, left)),
     )):
@@ -439,33 +463,66 @@
         )
         copy.start()
         ring.append(copy)
-    pad[0:5] = jnp.zeros((5, 8, 128), F32)
-    pad[15:20] = jnp.zeros((5, 8, 128), F32)
-
-    def a_arrive(k, total):
-        sender = lax.rem(px + k, GX)
-        a_copy(px, sender).wait_recv()
-        return total + part[GX + sender]
-
-    pad[5:15] = lax.fori_loop(1, GX, a_arrive, part[px])
-    offset = arow_ref[0] - 2 - H * py + 5
-
-    def b_start(j, c):
-        zy = lax.rem(py + j, GY)
-        first = jnp.clip(zy + offset, 0, 15)
-        for i in range(5):
-            send[zy, i] = pad[first + i]
-        b_copy(zy, py).start()
-        return c
-
-    lax.fori_loop(0, GY, b_start, 0)
-
+    start = jnp.clip(acol_ref[0] - 2 - W * px, -36, W) + 40
+
+    def all_rows(extra):
+        return pltpu.make_async_remote_copy(
+            src_ref=row_in.at[extra, pl.ds(0, GY - 1)], dst_ref=row_in.at[extra, pl.ds(0, GY - 1)],
+            send_sem=a_s.at[extra], recv_sem=a_r.at[extra], device_id=(0, py, px), device_id_type=MESH,
+        )
+
+    def windows_of(extra):
+        all_rows(extra).wait_recv()
+        row_pad[40:80] = jnp.sum(row_in[extra], axis=0)
+        for z in range(GX):
+            window_out[extra, z] = row_pad[pl.ds(start + 4 * z, 8)]
+
+    def b_copy(extra, z, zy, i):
+        return pltpu.make_async_remote_copy(
+            src_ref=window_out.at[extra, z], dst_ref=got.at[i, px], send_sem=b_s.at[0], recv_sem=b_r.at[i],
+            device_id=(1, zy, z), device_id_type=MESH,
+        )
+
+    def b_each(act):
+        def body(k, c):
+            z = lax.rem(px + k, GX)
+            for d in (-1, 0, 1, -2, 2):
+                zy = py + d
+                wanted = (zy >= 0) & (zy < GY)
+
+                @pl.when(wanted & far(zy, z) if d in (-2, 2) else wanted)
+                def _():
+                    act(b_copy(0, z, zy, 2 - d))
+
+            return c
+
+        lax.fori_loop(0, GX, body, 0)
+
+        def extra_body(k, c):
+            z = lax.rem(px + k, GX)
+            for at, targets in ((0, ((0, 1), (1, 0))), (GY - 1, ((GY - 1, 3), (GY - 2, 4)))):
+                @pl.when(py == at)
+                def _():
+                    for zy, i in targets:
+                        act(b_copy(1, z, zy, i))
+
+            return c
+
+        lax.fori_loop(0, GX, extra_body, 0)
+
+    windows_of(0)
+
+    @pl.when((py == 0) | (py == GY - 1))
+    def _():
+        windows_of(1)
+
+    b_each(lambda copy: copy.start())
     for copy in ring:
         copy.wait()
     g[0, 8:48] = ring_s[...]
     g[H + 1, 8:48] = ring_n[...]
     for r in range(H):
-        g[1 + r, 8:48] = pc[r, 40:80]
+        g[1 + r, 8:48] = rows[1 + r]
         g[1 + r, 7:8] = ring_w[r : r + 1]
         g[1 + r, 48:49] = ring_e[r : r + 1]
     for r in range(H):
@@ -492,18 +549,13 @@
     in_cols = (sub + col0 >= 0) & (sub + col0 < 32)
     first = jnp.clip(col0 + BOX0, 0, 88)
 
-    def a_sent(k, c):
-        a_copy(lax.rem(px + k, GX), px).wait_send()
-        return c
-
-    lax.fori_loop(1, GX, a_sent, 0)
-
-    def b_sent(zy, c):
-        b_copy(zy, py).wait_send()
-        return c
-
-    lax.fori_loop(0, GY, b_sent, 0)
-
+    all_rows(0).wait_send()
+    for t, to in ((0, 0), (GY + 1, GY - 1)):
+        @pl.when(py != to)
+        def _():
+            a_copy(t, 1, to).wait_send()
+
+    b_each(lambda copy: copy.wait_send())
     pltpu.make_async_remote_copy(
         src_ref=box, dst_ref=box, send_sem=c_s.at[0], recv_sem=c_r.at[0], device_id=(1, py, px), device_id_type=MESH
     ).wait_recv()
@@ -565,14 +617,15 @@
             VMEM((5, 128, 128), F32),
             VMEM((2, CHUNKS, 2, 2, 8, 128), F32),
             VMEM((2, CHUNKS, 2, 2, 8, 128), F32),
-            VMEM((GY, 5, 8, 128), F32),
+            VMEM((5, GX, 8, 128), F32),
             VMEM((4, 128), F32),
             VMEM((H * W, 128), F32),
-            VMEM((H, 120, 128), F32),
+            VMEM((H + 2, W, 128), F32),
             VMEM((2, 16, 128), F32),
-            VMEM((2 * GX, H, 8, 128), F32),
-            VMEM((20, 8, 128), F32),
-            VMEM((GY, 5, 8, 128), F32),
+            VMEM((GY + 2, W, 128), F32),
+            VMEM((2, GY, W, 128), F32),
+            VMEM((120, 128), F32),
+            VMEM((2, GX, 8, 128), F32),
             VMEM((H + 2, 56, 128), F32),
             VMEM((W, 128), F32),
             VMEM((W, 128), F32),
@@ -583,7 +636,7 @@
             VMEM((GY * GX, 4, 128), F32),
             VMEM((16, 144, 128), F32),
             dma((2, CHUNKS)), dma((2, CHUNKS)), dma((2, CHUNKS)), dma((2, CHUNKS)),
-            dma((GX,)), dma((GX,)), dma((4,)), dma((4,)), dma((GY,)), dma((GY,)), dma((1,)), dma((1,)),
+            dma((2,)), dma((2,)), dma((4,)), dma((4,)), dma((1,)), dma((5,)), dma((1,)), dma((1,)),
         ],
         compiler_params=pltpu.CompilerParams(collective_id=0, has_side_effects=True, vmem_limit_bytes=56291328),
     )(

time: 44.1 us -> 41.8 us (0.948)
  Pallas kernels: 40.4 us -> 38.1 us
    pallas_call x1, Pallas kernels: 40.4 us -> 38.1 us  [shards(): pl.pallas_call(kernel, name='step', out_shape=jax.ShapeDtypeStruct((H, W,...]
where the time goes in v4:
time: 41.8 us; the launch traced here: 41.6 us
  Pallas kernels  38.1 us (91%)
  between operations  1.97 us (5%)
  local copies, waits for them, and re-layouts  1.56 us (4%)
    pallas_call x1, Pallas kernels, shards(): pl.pallas_call(kernel, name='step', out_shape=jax.ShapeDtypeStruct((H, W,...  38.1 us

profile of v4, /device:TPU:1, one launch (start us, length us, event | category | flops | bytes accessed | tf_op | source)
XLA Modules:
  0.0 41.6 jit_solution(11275280276608325069)
XLA Ops:
  0.6 0.0 copy-start.1
  1.9 0.0 copy-done.1
  2.0 0.0 copy-start
  2.0 0.7 %copy-done = f32[1,60,60]{2,0,1:T(1,128)S(1)} copy-done((f32[1,60,60]{2,0,1:T(1,128)S(1)}, f32[1,60,60]{2,0,1:T(1,128)}, u32[]{:S(2)}) %copy-start) | copy-done | bytes 14424
  2.7 38.1 %step.1 = f32[10,40,128]{2,1,0:T(8,128)S(1)} custom-call(s32[1]{0:T(128)S(6)} %copy.8.arow_ref, s32[1]{0:T(128)S(6)} %copy.9.acol_ref, f32[10,40,60]{2,1,0:T(8,128)} %bitcast.20, f32[10,40,60]{2,1,0:T(8,128)} %bitcast.21, f32[10,2,40]{2,1,0:T(2,128)S(1)} %bitcast.19, f32[60,1,60]{2,1,0:T(1,128)S(1)} %bitcast.18), custom_call_target="tpu_custom_call" | custom-call | tf_op jit(solution)/shard_map/step/pallas_call | solution.py:592
  40.8 0.8 %slice_bitcast_fusion = (f32[1,60,10,40]{1,3,2,0:T(8,128)}, f32[1,60,10,40]{1,3,2,0:T(8,128)}) fusion(f32[10,40,128]{2,1,0:T(8,128)S(1)} %step.1), kind=kLoop, calls=%fused_computation | loop fusion | bytes 384000 | tf_op jit(solution)/shard_map/broadcast_in_dim | solution.py:647
Async XLA Ops:
  0.6 1.3 %copy-start.1 = (f32[1,2,10,40]{3,1,2,0:T(2,128)S(1)}, f32[1,2,10,40]{3,1,2,0:T(2,128)}, u32[]{:S(2)}) copy-start(f32[1,2,10,40]{3,1,2,0:T(2,128)} %param.8) | copy-start | bytes 9604
  2.0 0.8 %copy-start = (f32[1,60,60]{2,0,1:T(1,128)S(1)}, f32[1,60,60]{2,0,1:T(1,128)}, u32[]{:S(2)}) copy-start(f32[1,60,60]{2,0,1:T(1,128)} %param.9) | copy-start | bytes 43204

commit v5 on v4

--- a/solution.py
+++ b/solution.py
@@ -20,7 +20,7 @@
 SUB = 10
 CHUNKS = 4
 ROWS = 3 * H
-BLOCK = 6
+BLOCK = 4
 BOX0 = 56
 
 
@@ -87,10 +87,10 @@
         hello(grp, down, gx)
 
         def cross(j, c):
-            hello(0, lax.rem(gy + GY - 2 + j // GX, GY), lax.rem(gx + j, GX))
+            hello(0, gy, lax.rem(gx + j, GX))
             return c
 
-        lax.fori_loop(0, 5 * GX, cross, 0)
+        lax.fori_loop(0, GX, cross, 0)
 
     @pl.when(grp == 0)
     def _():
@@ -139,13 +139,14 @@
     low, high = k + 1, ROWS - 1 - k
     while low < high:
         n = min(BLOCK, high - low)
-        line = src[low : low + n]
+        tall = src[low - 1 : low + n + 1]
+        line = tall[1 : n + 1]
         dst[low : low + n] = (
             cfb[0, low : low + n] * line
             + cfb[1, low : low + n] * pltpu.roll(line, 127, 3)
             + cfb[2, low : low + n] * pltpu.roll(line, 1, 3)
-            + cfb[3, low : low + n] * src[low + 1 : low + n + 1]
-            + cfb[4, low : low + n] * src[low - 1 : low + n - 1]
+            + cfb[3, low : low + n] * tall[2:]
+            + cfb[4, low : low + n] * tall[:n]
         )
         low += n
 
@@ -427,7 +428,7 @@
     row_in[0, py] = row_out[py + 1]
     g[...] = jnp.zeros(g.shape, F32)
     row_pad[...] = jnp.zeros(row_pad.shape, F32)
-    pl.semaphore_wait(barrier, 5 * GX + GY - 1 + 2)
+    pl.semaphore_wait(barrier, GX + GY - 1 + 2)
 
     def a_copy(t, extra, to):
         return pltpu.make_async_remote_copy(

time: 41.8 us -> 39.9 us (0.955)
  Pallas kernels: 38.1 us -> 36.2 us
    pallas_call x1, Pallas kernels: 38.1 us -> 36.2 us  [shards(): pl.pallas_call(kernel, name='step', out_shape=jax.ShapeDtypeStruct((H, W,...]
where the time goes in v5:
time: 39.9 us; the launch traced here: 39.7 us
  Pallas kernels  36.2 us (91%)
  between operations  1.97 us (5%)
  local copies, waits for them, and re-layouts  1.56 us (4%)
    pallas_call x1, Pallas kernels, shards(): pl.pallas_call(kernel, name='step', out_shape=jax.ShapeDtypeStruct((H, W,...  36.2 us
    broadcast_in_dim x1, local copies, waits for them, and re-layouts, shards(): return tuple((half.transpose(2, 0, 1)[None] for half in both))  0.81 us

profile of v5, /device:TPU:1, one launch (start us, length us, event | category | flops | bytes accessed | tf_op | source)
XLA Modules:
  0.0 39.7 jit_solution(8532970397611156465)
XLA Ops:
  0.6 0.0 copy-start.1
  1.9 0.0 copy-done.1
  2.0 0.0 copy-start
  2.0 0.7 %copy-done = f32[1,60,60]{2,0,1:T(1,128)S(1)} copy-done((f32[1,60,60]{2,0,1:T(1,128)S(1)}, f32[1,60,60]{2,0,1:T(1,128)}, u32[]{:S(2)}) %copy-start) | copy-done | bytes 14424
  2.7 36.2 %step.1 = f32[10,40,128]{2,1,0:T(8,128)S(1)} custom-call(s32[1]{0:T(128)S(6)} %copy.8.arow_ref, s32[1]{0:T(128)S(6)} %copy.9.acol_ref, f32[10,40,60]{2,1,0:T(8,128)} %bitcast.20, f32[10,40,60]{2,1,0:T(8,128)} %bitcast.21, f32[10,2,40]{2,1,0:T(2,128)S(1)} %bitcast.19, f32[60,1,60]{2,1,0:T(1,128)S(1)} %bitcast.18), custom_call_target="tpu_custom_call" | custom-call | tf_op jit(solution)/shard_map/step/pallas_call | solution.py:593
  38.9 0.8 %slice_bitcast_fusion = (f32[1,60,10,40]{1,3,2,0:T(8,128)}, f32[1,60,10,40]{1,3,2,0:T(8,128)}) fusion(f32[10,40,128]{2,1,0:T(8,128)S(1)} %step.1), kind=kLoop, calls=%fused_computation | loop fusion | bytes 384000 | tf_op jit(solution)/shard_map/broadcast_in_dim | solution.py:648
Async XLA Ops:
  0.6 1.3 %copy-start.1 = (f32[1,2,10,40]{3,1,2,0:T(2,128)S(1)}, f32[1,2,10,40]{3,1,2,0:T(2,128)}, u32[]{:S(2)}) copy-start(f32[1,2,10,40]{3,1,2,0:T(2,128)} %param.8) | copy-start | bytes 9604
  2.0 0.8 %copy-start = (f32[1,60,60]{2,0,1:T(1,128)S(1)}, f32[1,60,60]{2,0,1:T(1,128)}, u32[]{:S(2)}) copy-start(f32[1,60,60]{2,0,1:T(1,128)} %param.9) | copy-start | bytes 43204

commit v6 on v5

--- a/solution.py
+++ b/solution.py
@@ -22,6 +22,8 @@
 ROWS = 3 * H
 BLOCK = 4
 BOX0 = 56
+EDGES = 2 * GX + 2 * (GY - 2)
+INNER = GY * GX - EDGES
 
 
 def dot(a, b):
@@ -56,9 +58,9 @@
     arow_ref, acol_ref, state_hbm, cot_hbm, faces_hbm, mix_hbm,
     out_ref,
     state, cot, faces, mixing, load_s, raw, mixed_rows, wide, square,
-    ya, yb, yc, yd, cf, cfb, en, bs, ss, power, strip_out, strip_in, got, msg,
-    cells, rows, ends, row_out, row_in, row_pad, window_out, g, ring_n, ring_s, ring_e, ring_w, faces_b, coarse, box, boxpad,
-    strip_s, strip_r, ns_s, ns_r, a_s, a_r, ring_snd, ring_rcv, b_s, b_r, c_s, c_r,
+    ya, yb, yc, yd, cf, cfb, en, bs, ss, power, strip_out, strip_in, face_out, face_in, got, msg, brief,
+    cells, rows, ends, row_out, row_in, extra_out, extra_in, row_pad, window_out, g, ring_n, ring_s, ring_e, ring_w, faces_b, coarse, box, inner, boxpad,
+    strip_s, strip_r, face_s, face_r, ns_s, ns_r, a_s, a_r, ring_snd, ring_rcv, b_s, b_r, c_s, c_r,
 ):
     grp = lax.axis_index("grp")
     gy = lax.axis_index("gy")
@@ -122,15 +124,15 @@
     def _():
         zoom(
             gy, gx, up, down, left, right, barrier, out_ref, state, cot, wide, mixed_rows, raw, square,
-            ya, yb, yc, yd, cf, cfb, en, bs, ss, power, strip_out, strip_in, got, msg, box,
-            strip_s, strip_r, ns_s, ns_r, b_s, b_r, c_s, c_r,
+            ya, yb, yc, yd, cf, cfb, en, bs, ss, power, strip_out, strip_in, face_out, face_in, got, msg, brief, box, inner,
+            strip_s, strip_r, face_s, face_r, ns_s, ns_r, b_s, b_r, c_s, c_r,
         )
 
     @pl.when(grp == 0)
     def _():
         parent(
             gy, gx, up, down, left, right, barrier, arow_ref, acol_ref, out_ref, state, cot, wide, square,
-            cells, rows, ends, row_out, row_in, row_pad, window_out, got, g, ring_n, ring_s, ring_e, ring_w, faces_b, coarse, msg, box, boxpad,
+            cells, rows, ends, row_out, row_in, extra_out, extra_in, row_pad, window_out, got, g, ring_n, ring_s, ring_e, ring_w, faces_b, coarse, box, inner, boxpad,
             a_s, a_r, ring_snd, ring_rcv, b_s, b_r, c_s, c_r,
         )
 
@@ -161,8 +163,8 @@
 
 def zoom(
     zy, zx, up, down, left, right, barrier, out_ref, state, cot, wide, mixed_rows, raw, square,
-    ya, yb, yc, yd, cf, cfb, en, bs, ss, power, strip_out, strip_in, got, msg, box,
-    strip_s, strip_r, ns_s, ns_r, b_s, b_r, c_s, c_r,
+    ya, yb, yc, yd, cf, cfb, en, bs, ss, power, strip_out, strip_in, face_out, face_in, got, msg, brief, box, inner,
+    strip_s, strip_r, face_s, face_r, ns_s, ns_r, b_s, b_r, c_s, c_r,
 ):
     lane = iota((64, 128), 1)
     lane64 = lane % 64
@@ -200,6 +202,12 @@
             device_id=(1, (up, down)[s], zx), device_id_type=MESH,
         )
 
+    def face_copy(s):
+        return pltpu.make_async_remote_copy(
+            src_ref=face_out, dst_ref=face_in.at[s], send_sem=face_s.at[s], recv_sem=face_r.at[s],
+            device_id=(1, (up, down)[s], zx), device_id_type=MESH,
+        )
+
     order = (3, 0, 1, 2)
     for c in order:
         for s in range(2):
@@ -217,6 +225,11 @@
                 here = (lane16 % 64 >= 50) & (lane16 % 64 < 60)
                 row = jnp.where(here, pltpu.roll(from_east, (50 - 10 * k) % 128, 2), row)
                 ya[c, H + 5 * q + k] = row
+        if c == 3:
+            for r in range(H):
+                face_out[r] = ya[3, H + r, 1, 4:6]
+            for s in range(2):
+                face_copy(s).start()
         for s in range(2):
             end_copy(s, c).start()
 
@@ -263,11 +276,13 @@
             yc[r, b] = value + tan_slot if b == 0 else value
 
     for s in range(2):
-        end_copy(s, 3).wait()
+        face_copy(s).wait()
     for i in range(2):
         en[i] = jnp.zeros((48, 128), F32)
-        for r in range(ROWS):
-            en[i, 8 + r : 9 + r] = ya[3, r, 1, 4 + i : 5 + i]
+        for r in range(H):
+            en[i, 8 + r : 9 + r] = face_in[0, r, i : i + 1]
+            en[i, 8 + H + r : 9 + H + r] = face_out[r, i : i + 1]
+            en[i, 8 + 2 * H + r : 9 + 2 * H + r] = face_in[1, r, i : i + 1]
     east = en[0, 8:38]
     west = pltpu.roll(east, 1, 1)
     north = en[1, 8:38]
@@ -291,10 +306,8 @@
     def chunk(i, carry):
         c = lax.rem(i + 3, CHUNKS)
 
-        @pl.when(i > 0)
-        def _():
-            for s in range(2):
-                end_copy(s, c).wait()
+        for s in range(2):
+            end_copy(s, c).wait()
 
         for k in range(SUB):
             src, dst = (ya.at[c], yb) if k % 2 == 0 else (yb, ya.at[c])
@@ -366,17 +379,37 @@
     q = dot(jnp.concatenate(p[1::2], 0), power[1])
     q = [p[2 * i] + q[8 * i : 8 * i + 8] for i in range(3)]
     line = q[0] + dot(q[1], power[2]) + dot(q[2], power[3])
-    msg[...] = line[0:4]
-    me = zy * GX + zx
-
-    def c_start(i, c):
-        pltpu.make_async_remote_copy(
-            src_ref=msg, dst_ref=box.at[me], send_sem=c_s.at[0], recv_sem=c_r.at[0],
-            device_id=(0, lax.rem(zy + i // GX, GY), lax.rem(zx + i, GX)), device_id_type=MESH,
-        ).start()
-        return c
-
-    lax.fori_loop(0, GY * GX, c_start, 0, unroll=8)
+    swapped = pltpu.roll(line, 64, 1)
+    on_edge = (zy == 0) | (zy == GY - 1) | (zx == 0) | (zx == GX - 1)
+
+    def c_copy(src, dst, kind, i):
+        return pltpu.make_async_remote_copy(
+            src_ref=src, dst_ref=dst, send_sem=c_s.at[kind], recv_sem=c_r.at[kind],
+            device_id=(0, (zy + (i >> 3)) & (GY - 1), (zx + i) & (GX - 1)), device_id_type=MESH,
+        )
+
+    @pl.when(on_edge)
+    def _():
+        msg[...] = line[0:4]
+        side = 2 * GX + 2 * (zy - 1) + jnp.where(zx == 0, 0, 1)
+        at = jnp.where(zy == 0, zx, jnp.where(zy == GY - 1, GX + zx, side))
+
+        def c_start(i, c):
+            c_copy(msg, box.at[at], 0, i).start()
+            return c
+
+        lax.fori_loop(0, GY * GX, c_start, 0, unroll=8)
+
+    @pl.when(jnp.logical_not(on_edge))
+    def _():
+        brief[...] = jnp.where(lane8 < 64, line, jnp.concatenate([swapped[2:4], swapped[0:6]], 0))[0:2]
+        at = (GX - 2) * (zy - 1) + zx - 1
+
+        def c_start(i, c):
+            c_copy(brief, inner.at[at], 1, i).start()
+            return c
+
+        lax.fori_loop(0, GY * GX, c_start, 0, unroll=8)
 
     powers = jnp.concatenate([v0, dot(v0, power[0])], 0)
     last = dot(powers, power[3])
@@ -396,14 +429,19 @@
     for c in order:
         for s in range(2):
             strip_copy(s, c).wait_send()
-    pltpu.make_async_remote_copy(
-        src_ref=box, dst_ref=box, send_sem=c_s.at[0], recv_sem=c_r.at[0], device_id=(0, zy, zx), device_id_type=MESH
-    ).wait_send()
+
+    @pl.when(on_edge)
+    def _():
+        c_copy(power.at[pl.ds(0, 4)], power.at[pl.ds(0, 4)], 0, 0).wait_send()
+
+    @pl.when(jnp.logical_not(on_edge))
+    def _():
+        c_copy(power.at[pl.ds(0, 2)], power.at[pl.ds(0, 2)], 1, 0).wait_send()
 
 
 def parent(
     py, px, up, down, left, right, barrier, arow_ref, acol_ref, out_ref, state, cot, wide, square,
-    cells, rows, ends, row_out, row_in, row_pad, window_out, got, g, ring_n, ring_s, ring_e, ring_w, faces_b, coarse, msg, box, boxpad,
+    cells, rows, ends, row_out, row_in, extra_out, extra_in, row_pad, window_out, got, g, ring_n, ring_s, ring_e, ring_w, faces_b, coarse, box, inner, boxpad,
     a_s, a_r, ring_snd, ring_rcv, b_s, b_r, c_s, c_r,
 ):
     r128 = iota((128, 128), 0)
@@ -425,32 +463,40 @@
         ends[1, r : r + 1] = rows[1 + r, W - 1 : W]
     for t in range(GY + 2):
         row_out[t] = rows[jnp.clip(t - 1 + arow_ref[0] - H * py, -1, H) + 1]
-    row_in[0, py] = row_out[py + 1]
+    row_in[py] = row_out[py + 1]
+    lane24 = iota((24, 128), 1)
+    for s, t in enumerate((0, GY + 1)):
+        extra_out[s] = jnp.where(lane24 < 64, row_out[t, 0:24], pltpu.roll(row_out[t, 16:40], 64, 1))
     g[...] = jnp.zeros(g.shape, F32)
     row_pad[...] = jnp.zeros(row_pad.shape, F32)
     pl.semaphore_wait(barrier, GX + GY - 1 + 2)
 
-    def a_copy(t, extra, to):
+    def a_copy(to):
         return pltpu.make_async_remote_copy(
-            src_ref=row_out.at[t], dst_ref=row_in.at[extra, py], send_sem=a_s.at[extra], recv_sem=a_r.at[extra],
+            src_ref=row_out.at[to + 1], dst_ref=row_in.at[py], send_sem=a_s.at[0], recv_sem=a_r.at[0],
             device_id=(0, to, px), device_id_type=MESH,
         )
 
+    def x_copy(s):
+        return pltpu.make_async_remote_copy(
+            src_ref=extra_out.at[s], dst_ref=extra_in.at[py], send_sem=a_s.at[1 + s], recv_sem=a_r.at[1],
+            device_id=(0, 2 * px + s, px), device_id_type=MESH,
+        )
+
     def a_start(k, c):
-        to = lax.rem(py + k, GY)
-        a_copy(to + 1, 0, to).start()
+        a_copy((py + k) & (GY - 1)).start()
         return c
 
-    for t, to in ((0, 0), (GY + 1, GY - 1)):
-        @pl.when(py != to)
+    for s in range(2):
+        @pl.when(py != 2 * px + s)
         def _():
-            a_copy(t, 1, to).start()
-
-        @pl.when(py == to)
+            x_copy(s).start()
+
+        @pl.when(py == 2 * px + s)
         def _():
-            row_in[1, to] = row_out[t]
-
-    lax.fori_loop(1, GY, a_start, 0)
+            extra_in[py] = extra_out[s]
+
+    lax.fori_loop(1, GY, a_start, 0, unroll=5)
     ring = []
     for s, (src, dst, where) in enumerate((
         (rows.at[H], ring_s, (0, up, px)),
@@ -466,15 +512,13 @@
         ring.append(copy)
     start = jnp.clip(acol_ref[0] - 2 - W * px, -36, W) + 40
 
-    def all_rows(extra):
+    def all_rows(ref, i):
         return pltpu.make_async_remote_copy(
-            src_ref=row_in.at[extra, pl.ds(0, GY - 1)], dst_ref=row_in.at[extra, pl.ds(0, GY - 1)],
-            send_sem=a_s.at[extra], recv_sem=a_r.at[extra], device_id=(0, py, px), device_id_type=MESH,
-        )
-
-    def windows_of(extra):
-        all_rows(extra).wait_recv()
-        row_pad[40:80] = jnp.sum(row_in[extra], axis=0)
+            src_ref=ref.at[pl.ds(0, GY - 1)], dst_ref=ref.at[pl.ds(0, GY - 1)],
+            send_sem=a_s.at[i], recv_sem=a_r.at[i], device_id=(0, py, px), device_id_type=MESH,
+        )
+
+    def cut(extra):
         for z in range(GX):
             window_out[extra, z] = row_pad[pl.ds(start + 4 * z, 8)]
 
@@ -486,7 +530,7 @@
 
     def b_each(act):
         def body(k, c):
-            z = lax.rem(px + k, GX)
+            z = (px + k) & (GX - 1)
             for d in (-1, 0, 1, -2, 2):
                 zy = py + d
                 wanted = (zy >= 0) & (zy < GY)
@@ -497,12 +541,12 @@
 
             return c
 
-        lax.fori_loop(0, GX, body, 0)
+        lax.fori_loop(0, GX, body, 0, unroll=4)
 
         def extra_body(k, c):
-            z = lax.rem(px + k, GX)
-            for at, targets in ((0, ((0, 1), (1, 0))), (GY - 1, ((GY - 1, 3), (GY - 2, 4)))):
-                @pl.when(py == at)
+            z = (px + k) & (GX - 1)
+            for s, targets in enumerate((((0, 1), (1, 0)), ((GY - 1, 3), (GY - 2, 4)))):
+                @pl.when(py == 2 * px + s)
                 def _():
                     for zy, i in targets:
                         act(b_copy(1, z, zy, i))
@@ -511,11 +555,17 @@
 
         lax.fori_loop(0, GX, extra_body, 0)
 
-    windows_of(0)
-
-    @pl.when((py == 0) | (py == GY - 1))
-    def _():
-        windows_of(1)
+    all_rows(row_in, 0).wait_recv()
+    row_pad[40:80] = jnp.sum(row_in[...], axis=0)
+    cut(0)
+
+    @pl.when((py == 2 * px) | (py == 2 * px + 1))
+    def _():
+        all_rows(extra_in, 1).wait_recv()
+        both = jnp.sum(extra_in[...], axis=0)
+        row_pad[40:64] = jnp.where(lane24 < 64, both, F32(0.0))
+        row_pad[64:80] = jnp.where(lane24 < 64, pltpu.roll(both, 64, 1), F32(0.0))[8:24]
+        cut(1)
 
     b_each(lambda copy: copy.start())
     for copy in ring:
@@ -550,19 +600,29 @@
     in_cols = (sub + col0 >= 0) & (sub + col0 < 32)
     first = jnp.clip(col0 + BOX0, 0, 88)
 
-    all_rows(0).wait_send()
-    for t, to in ((0, 0), (GY + 1, GY - 1)):
-        @pl.when(py != to)
+    all_rows(row_in, 0).wait_send()
+    for s in range(2):
+        @pl.when(py != 2 * px + s)
         def _():
-            a_copy(t, 1, to).wait_send()
+            x_copy(s).wait_send()
 
     b_each(lambda copy: copy.wait_send())
-    pltpu.make_async_remote_copy(
-        src_ref=box, dst_ref=box, send_sem=c_s.at[0], recv_sem=c_r.at[0], device_id=(1, py, px), device_id_type=MESH
-    ).wait_recv()
+    for i, ref in enumerate((box, inner)):
+        pltpu.make_async_remote_copy(
+            src_ref=ref, dst_ref=ref, send_sem=c_s.at[i], recv_sem=c_r.at[i], device_id=(1, py, px), device_id_type=MESH
+        ).wait_recv()
+    lane2 = iota((2, 128), 1)
     for i in range(16):
         for z in range(GX):
-            boxpad[i, BOX0 + 4 * z : BOX0 + 4 + 4 * z] = box[GX * i + z]
+            to = BOX0 + 4 * z
+            if i in (0, 15):
+                boxpad[i, to : to + 4] = box[z + (GX if i else 0)]
+            elif z in (0, GX - 1):
+                boxpad[i, to : to + 4] = box[2 * GX + 2 * (i - 1) + (1 if z else 0)]
+            else:
+                pair = inner[(GX - 2) * (i - 1) + z - 1]
+                boxpad[i, to : to + 2] = jnp.where(lane2 < 64, pair, F32(0.0))
+                boxpad[i, to + 2 : to + 4] = jnp.where(lane2 < 64, pltpu.roll(pair, 64, 1), F32(0.0))
     windows = []
     for i in range(H + 2):
         br = row0 + i
@@ -618,13 +678,18 @@
             VMEM((5, 128, 128), F32),
             VMEM((2, CHUNKS, 2, 2, 8, 128), F32),
             VMEM((2, CHUNKS, 2, 2, 8, 128), F32),
+            VMEM((H, 2, 128), F32),
+            VMEM((2, H, 2, 128), F32),
             VMEM((5, GX, 8, 128), F32),
             VMEM((4, 128), F32),
+            VMEM((2, 128), F32),
             VMEM((H * W, 128), F32),
             VMEM((H + 2, W, 128), F32),
             VMEM((2, 16, 128), F32),
             VMEM((GY + 2, W, 128), F32),
-            VMEM((2, GY, W, 128), F32),
+            VMEM((GY, W, 128), F32),
+            VMEM((2, 24, 128), F32),
+            VMEM((GY, 24, 128), F32),
             VMEM((120, 128), F32),
             VMEM((2, GX, 8, 128), F32),
             VMEM((H + 2, 56, 128), F32),
@@ -634,10 +699,11 @@
             VMEM((16, 128), F32),
             VMEM((4, H, 56, 128), F32),
             VMEM((H, 56, 128), F32),
-            VMEM((GY * GX, 4, 128), F32),
+            VMEM((EDGES, 4, 128), F32),
+            VMEM((INNER, 2, 128), F32),
             VMEM((16, 144, 128), F32),
-            dma((2, CHUNKS)), dma((2, CHUNKS)), dma((2, CHUNKS)), dma((2, CHUNKS)),
-            dma((2,)), dma((2,)), dma((4,)), dma((4,)), dma((1,)), dma((5,)), dma((1,)), dma((1,)),
+            dma((2, CHUNKS)), dma((2, CHUNKS)), dma((2,)), dma((2,)), dma((2, CHUNKS)), dma((2, CHUNKS)),
+            dma((3,)), dma((2,)), dma((4,)), dma((4,)), dma((1,)), dma((5,)), dma((2,)), dma((2,)),
         ],
         compiler_params=pltpu.CompilerParams(collective_id=0, has_side_effects=True, vmem_limit_bytes=56291328),
     )(

time: 39.9 us -> 39.7 us (level)
  no operation moved by 1% of the time
where the time goes in v6:
time: 39.7 us; the launch traced here: 39.5 us
  Pallas kernels  36 us (91%)
  between operations  1.97 us (5%)
  local copies, waits for them, and re-layouts  1.56 us (4%)
    pallas_call x1, Pallas kernels, shards(): pl.pallas_call(kernel, name='step', out_shape=jax.ShapeDtypeStruct((H, W,...  36 us
    broadcast_in_dim x1, local copies, waits for them, and re-layouts, shards(): return tuple((half.transpose(2, 0, 1)[None] for half in both))  0.81 us

profile of v6, /device:TPU:1, one launch (start us, length us, event | category | flops | bytes accessed | tf_op | source)
XLA Modules:
  0.0 39.5 jit_solution(7295151358286999766)
XLA Ops:
  0.6 0.0 copy-start.1
  1.9 0.0 copy-done.1
  2.0 0.0 copy-start
  2.0 0.7 %copy-done = f32[1,60,60]{2,0,1:T(1,128)S(1)} copy-done((f32[1,60,60]{2,0,1:T(1,128)S(1)}, f32[1,60,60]{2,0,1:T(1,128)}, u32[]{:S(2)}) %copy-start) | copy-done | bytes 14424
  2.7 36.0 %step.1 = f32[10,40,128]{2,1,0:T(8,128)S(1)} custom-call(s32[1]{0:T(128)S(6)} %copy.8.arow_ref, s32[1]{0:T(128)S(6)} %copy.9.acol_ref, f32[10,40,60]{2,1,0:T(8,128)} %bitcast.20, f32[10,40,60]{2,1,0:T(8,128)} %bitcast.21, f32[10,2,40]{2,1,0:T(2,128)S(1)} %bitcast.19, f32[60,1,60]{2,1,0:T(1,128)S(1)} %bitcast.18), custom_call_target="tpu_custom_call" | custom-call | tf_op jit(solution)/shard_map/step/pallas_call | solution.py:653
  38.7 0.8 %slice_bitcast_fusion = (f32[1,60,10,40]{1,3,2,0:T(8,128)}, f32[1,60,10,40]{1,3,2,0:T(8,128)}) fusion(f32[10,40,128]{2,1,0:T(8,128)S(1)} %step.1), kind=kLoop, calls=%fused_computation | loop fusion | bytes 384000 | tf_op jit(solution)/shard_map/broadcast_in_dim | solution.py:714
Async XLA Ops:
  0.6 1.3 %copy-start.1 = (f32[1,2,10,40]{3,1,2,0:T(2,128)S(1)}, f32[1,2,10,40]{3,1,2,0:T(2,128)}, u32[]{:S(2)}) copy-start(f32[1,2,10,40]{3,1,2,0:T(2,128)} %param.8) | copy-start | bytes 9604
  2.0 0.8 %copy-start = (f32[1,60,60]{2,0,1:T(1,128)S(1)}, f32[1,60,60]{2,0,1:T(1,128)}, u32[]{:S(2)}) copy-start(f32[1,60,60]{2,0,1:T(1,128)} %param.9) | copy-start | bytes 43204

commit v7 on v6

--- a/solution.py
+++ b/solution.py
@@ -303,6 +303,11 @@
         ss[k, 11:16] = jnp.zeros((5, 8, 128), F32)
         sweep(src, dst, cfb, k)
 
+    pick_tan = only((lane8 >= 10) & (lane8 < 50) & (lane8 // 10 - 1 == sub8), 0.01)
+    slot_sum = jnp.sum(bs[...], axis=0).reshape(8 * SUB, 128)
+    means = dot_t(pick_tan, jnp.concatenate([slot_sum, jnp.zeros((48, 128), F32)], 0))
+    means = jnp.concatenate([pltpu.roll(means, (-8 * k) % 128, 1) for k in range(SUB)], 0)
+
     def chunk(i, carry):
         c = lax.rem(i + 3, CHUNKS)
 
@@ -317,15 +322,11 @@
 
     lax.fori_loop(0, CHUNKS, chunk, 0)
 
-    pick_tan = only((lane8 >= 10) & (lane8 < 50) & (lane8 // 10 - 1 == sub8), 0.01)
     pick_adj = only((lane8 >= 74) & (lane8 < 114) & ((lane8 - 64) // 10 - 1 == sub8))
     sums = dot_t(pick_adj, ss[...].reshape(SUB * 128, 128))
     sums = lanes_to_rows(sums, SUB)
     lane80 = iota((8 * SUB, 128), 1)
     level_sum = jnp.sum(ya[:, H : 2 * H], axis=1).reshape(64, 128)
-    slot_sum = jnp.sum(bs[...], axis=0).reshape(8 * SUB, 128)
-    means = dot_t(pick_tan, jnp.concatenate([slot_sum, jnp.zeros((48, 128), F32)], 0))
-    means = jnp.concatenate([pltpu.roll(means, (-8 * k) % 128, 1) for k in range(SUB)], 0)
     weights = jnp.where(lane80 < 32, jnp.where(lane80 < 8, means, pltpu.roll(sums, 72, 1)), F32(0.0))
     own_sums = pltpu.roll(jnp.where(lane80 < L, sums, F32(0.0)), 64, 1)
     own_mean = dot_t(pick_tan, padded_rows(level_sum, 128))

time: 39.7 us -> 39.7 us (level)
  no operation moved by 1% of the time
where the time goes in v7:
time: 39.7 us; the launch traced here: 39.5 us
  Pallas kernels  36 us (91%)
  between operations  1.97 us (5%)
  local copies, waits for them, and re-layouts  1.56 us (4%)
    pallas_call x1, Pallas kernels, shards(): pl.pallas_call(kernel, name='step', out_shape=jax.ShapeDtypeStruct((H, W,...  36 us
    broadcast_in_dim x1, local copies, waits for them, and re-layouts, shards(): return tuple((half.transpose(2, 0, 1)[None] for half in both))  0.81 us

profile of v7, /device:TPU:1, one launch (start us, length us, event | category | flops | bytes accessed | tf_op | source)
XLA Modules:
  0.0 39.5 jit_solution(4712932389622623239)
XLA Ops:
  0.6 0.0 copy-start.1
  1.9 0.0 copy-done.1
  2.0 0.0 copy-start
  2.0 0.7 %copy-done = f32[1,60,60]{2,0,1:T(1,128)S(1)} copy-done((f32[1,60,60]{2,0,1:T(1,128)S(1)}, f32[1,60,60]{2,0,1:T(1,128)}, u32[]{:S(2)}) %copy-start) | copy-done | bytes 14424
  2.7 36.0 %step.1 = f32[10,40,128]{2,1,0:T(8,128)S(1)} custom-call(s32[1]{0:T(128)S(6)} %copy.8.arow_ref, s32[1]{0:T(128)S(6)} %copy.9.acol_ref, f32[10,40,60]{2,1,0:T(8,128)} %bitcast.20, f32[10,40,60]{2,1,0:T(8,128)} %bitcast.21, f32[10,2,40]{2,1,0:T(2,128)S(1)} %bitcast.19, f32[60,1,60]{2,1,0:T(1,128)S(1)} %bitcast.18), custom_call_target="tpu_custom_call" | custom-call | tf_op jit(solution)/shard_map/step/pallas_call | solution.py:654
  38.7 0.8 %slice_bitcast_fusion = (f32[1,60,10,40]{1,3,2,0:T(8,128)}, f32[1,60,10,40]{1,3,2,0:T(8,128)}) fusion(f32[10,40,128]{2,1,0:T(8,128)S(1)} %step.1), kind=kLoop, calls=%fused_computation | loop fusion | bytes 384000 | tf_op jit(solution)/shard_map/broadcast_in_dim | solution.py:715
Async XLA Ops:
  0.6 1.3 %copy-start.1 = (f32[1,2,10,40]{3,1,2,0:T(2,128)S(1)}, f32[1,2,10,40]{3,1,2,0:T(2,128)}, u32[]{:S(2)}) copy-start(f32[1,2,10,40]{3,1,2,0:T(2,128)} %param.8) | copy-start | bytes 9604
  2.0 0.8 %copy-start = (f32[1,60,60]{2,0,1:T(1,128)S(1)}, f32[1,60,60]{2,0,1:T(1,128)}, u32[]{:S(2)}) copy-start(f32[1,60,60]{2,0,1:T(1,128)} %param.9) | copy-start | bytes 43204
